TPU v7x, 512 devices: a whole 4x8x8 slice. The times are simulated.
512 devices in a mesh: ctx: 128 (over y, z, core), head: 4 (over x).
Axes of the slice: x: 4, y: 8, z: 8, core: 2. Of those that a mesh axis runs over, the one named last changes fastest.
Arguments:
- queries: bfloat16 [16384, 3072], P(('ctx', 'head')), may hold values from -28 to 28, as said below
- keys: bfloat16 [16384, 3072], P(('ctx', 'head')), may hold values from -14 to 14
- values: bfloat16 [16384, 3072], P(('ctx', 'head')), may hold values from -6 to 6
- band_offsets: int32 [7], replicated, may hold values from -2 to 2
- band_widths: int32 [7], replicated, may hold values from 1 to 4
- block_mask: int32 [7, 8], replicated, may hold values 0 or 1
Outputs:
- attended: bfloat16 [16384, 3072], P(('ctx', 'head'))
Inputs may be any that keep to these rules, and one draw needn't show every extreme that they name: `queries`: queries and keys of one head are of order one in most rows.
All inputs are finite; a program needn't handle non-finite values.
Results may differ from a plain program's by a relative error of at most 0.0046.
Values may be sent and summed in bfloat16 or wider, within the bound.
A program may use at most 64 MiB of HBM per device.

v0:
```python
import jax
import jax.numpy as jnp
from jax import lax
from jax.sharding import PartitionSpec as P

HD = 128
BLOCKS = 8
NBANDS = 7


NEG = -1e30


def shifted(block, axis, distance):
    devices = range(lax.axis_size(axis))
    route = [(i - distance, i) for i in devices if i - distance in devices]
    return lax.ppermute(block, axis, route)


def block_rule(band_index, band_offsets, band_widths, block_mask, row_count):
    block_rows = row_count // BLOCKS
    query_block = lax.iota(jnp.int32, row_count) // block_rows
    onehot_rows = (query_block[:, None] == lax.iota(jnp.int32, BLOCKS)[None, :]).astype(jnp.int32)
    row_active = jnp.sum(onehot_rows * block_mask[band_index][None, :], axis=1)
    distance = query_block[None, :] - query_block[:, None] - band_offsets[band_index]
    allowed = (row_active[:, None] == 1) & (jnp.abs(distance) < band_widths[band_index])
    if band_index == 0:
        allowed = allowed | (query_block[:, None] == query_block[None, :])
    return allowed


def on_device(queries, keys, values, band_offsets, band_widths, block_mask):
    local_queries, local_keys, local_values = (
        lax.all_to_all(queries, "head", split_axis=1, concat_axis=0, tiled=True),
        lax.all_to_all(keys, "head", split_axis=1, concat_axis=0, tiled=True),
        lax.all_to_all(values, "head", split_axis=1, concat_axis=0, tiled=True),
    )
    row_count = local_queries.shape[0]
    feature_count = local_queries.shape[1]
    head_count = feature_count // HD
    frame_index = lax.axis_index("ctx")
    frame_total = lax.axis_size("ctx")
    paired = jnp.concatenate([local_keys, local_values], axis=1)
    entries = [(paired, 0, jnp.array(True))]
    earlier = shifted(paired, "ctx", 1)
    later = shifted(paired, "ctx", -1)
    entries.append((earlier, 1, frame_index >= 1))
    entries.append((later, 1, frame_index + 1 < frame_total))
    for band_index in range(2, NBANDS):
        reach = 2 ** (band_index - 1)
        earlier = shifted(paired, "ctx", reach)
        later = shifted(paired, "ctx", -reach)
        entries.append((earlier, band_index, frame_index >= reach))
        entries.append((later, band_index, frame_index + reach < frame_total))
    scale = HD ** (-0.5)
    query_heads = local_queries.reshape(row_count, head_count, HD)

    def masked_scores(entry):
        paired_keys, band_index, valid = entry
        key_heads = paired_keys[:, :feature_count].reshape(row_count, head_count, HD)
        scores = (
            jnp.einsum("qhd,khd->hqk", query_heads, key_heads, preferred_element_type=jnp.float32)
            * scale
        )
        allowed = block_rule(band_index, band_offsets, band_widths, block_mask, row_count) & valid
        return (jnp.where(allowed[None], scores, NEG), allowed)

    kept = [masked_scores(entry) for entry in entries]
    peak = kept[0][0].max(axis=-1)
    for scores, allowed in kept[1:]:
        peak = jnp.maximum(peak, scores.max(axis=-1))
    total = jnp.zeros((head_count, row_count), jnp.float32)
    summed = jnp.zeros((row_count, head_count, HD), jnp.float32)
    for position in range(len(entries)):
        scores, allowed = kept[position]
        weight = jnp.where(allowed[None], jnp.exp(scores - peak[..., None]), 0.0)
        total = total + weight.sum(axis=-1)
        value_heads = entries[position][0][:, feature_count:].reshape(row_count, head_count, HD)
        summed = summed + jnp.einsum(
            "hqk,khd->qhd",
            weight.astype(jnp.bfloat16),
            value_heads,
            preferred_element_type=jnp.float32,
        )
    result = (
        (summed / jnp.transpose(total)[:, :, None])
        .reshape(row_count, feature_count)
        .astype(jnp.bfloat16)
    )
    return lax.all_to_all(result, "head", split_axis=0, concat_axis=1, tiled=True)


def solution(mesh):
    return jax.shard_map(
        on_device,
        mesh=mesh,
        in_specs=(
            P(("ctx", "head"), None),
            P(("ctx", "head"), None),
            P(("ctx", "head"), None),
            P(),
            P(),
            P(),
        ),
        out_specs=P(("ctx", "head"), None),
        check_vma=False,
    )
```

profile of v0, /device:TPU:96, one launch (start us, length us, event | category | flops | bytes accessed | tf_op | source)
XLA Modules:
  0.0 192.2 jit_solution(7461805587499891247)
XLA Ops:
  1.6 4.4 %all-to-all-start.2 = ((bf16[32,4,768]{2,0,1:T(8,128)(2,1)}), bf16[32,4,768]{2,0,1:T(8,128)(2,1)S(1)}, u32[]{:S(2)}, u32[]{:S(2)}) async-start(bf16[32,4,768]{2,0,1:T(8,128)(2,1)} %bitcast.212), calls=%async_computation.2 | async-start | bytes 393216 | tf_op jit(solution)/shard_map/all_to_all | solution.py:36
  10.6 5.7 %broadcast_and_fusion.11 = (pred[128,128]{0,1:T(8,128)(4,1)S(1)}, pred[128,128]{0,1:T(8,128)(4,1)S(1)}, pred[128,128]{0,1:T(8,128)(4,1)}, pred[128,128]{0,1:T(8,...) fusion(pred[]{:T(512)S(6)} %ge.18, s32[]{:T(128)} %bitcast.7, ...), kind=kLoop, calls=%fused_computation.189 | loop fusion | flops 409600 | bytes 115750 | tf_op jit(solution)/shard_map/and | solution.py:65
  16.3 4.8 %all-to-all-start.1 = ((bf16[32,4,768]{2,0,1:T(8,128)(2,1)}), bf16[32,4,768]{2,0,1:T(8,128)(2,1)S(1)}, u32[]{:S(2)}, u32[]{:S(2)}) async-start(bf16[32,4,768]{2,0,1:T(8,128)(2,1)} %bitcast.213), calls=%async_computation.1 | async-start | bytes 393216 | tf_op jit(solution)/shard_map/all_to_all | solution.py:35
  21.1 6.3 %all-to-all-done.1 = bf16[32,4,768]{2,0,1:T(8,128)(2,1)S(1)} async-done(((bf16[32,4,768]{2,0,1:T(8,128)(2,1)}), bf16[32,4,768]{2,0,1:T(8,128)(2,1)S(1)}, u32[]{:S(2)}, u32[]{:S(2)}) %all-to-all-start.1) | async-done | bytes 196640 | tf_op jit(solution)/shard_map/all_to_all | solution.py:35
  27.4 3.4 %all-to-all-start = ((bf16[32,4,768]{2,0,1:T(8,128)(2,1)}), bf16[32,4,768]{2,0,1:T(8,128)(2,1)S(1)}, u32[]{:S(2)}, u32[]{:S(2)}) async-start(bf16[32,4,768]{2,0,1:T(8,128)(2,1)} %bitcast.214), calls=%async_computation | async-start | bytes 393216 | tf_op jit(solution)/shard_map/all_to_all | solution.py:34
  31.6 1.9 collective-permute-start.1
  33.5 4.6 %broadcast_and_fusion.9 = (pred[128,128]{0,1:T(8,128)(4,1)S(1)}, pred[128,128]{0,1:T(8,128)(4,1)}, pred[128,128]{0,1:T(8,128)(4,1)S(1)}, pred[128,128]{0,1:T(8,1...) fusion(pred[]{:T(512)S(6)} %ge.19, s32[]{:T(128)} %bitcast.17, s32[]{:T(128)} %bitcast.16, ...), kind=kLoop, calls=%fused_computation.187 | loop fusion | flops 311296 | bytes 99230 | tf_op jit(solution)/shard_map/and | solution.py:65
  38.1 2.4 %collective-permute-start = (bf16[128,1536]{1,0:T(8,128)(2,1)}, bf16[128,1536]{1,0:T(8,128)(2,1)S(1)}, u32[]{:S(2)}, u32[]{:S(2)}) collective-permute-start(bf16[128,1536]{1,0:T(8,128)(2,1)} %pad_maximum_fusion), channel_id=1, source_target_pairs={{0,4},{4,8},{8,12},{12,16},{16,20},{20,24},{24,28},{28,32},{32,36}... | collective-permute-start | bytes 1179656 | tf_op jit(solution)/shard_map/ppermute | solution.py:17
  40.5 2.2 %collective-permute-start.11 = (bf16[128,1536]{1,0:T(8,128)(2,1)}, bf16[128,1536]{1,0:T(8,128)(2,1)}, u32[]{:S(2)}, u32[]{:S(2)}) collective-permute-start(bf16[128,1536]{1,0:T(8,128)(2,1)} %pad_maximum_fusion), channel_id=1, source_target_pairs={{128,0},{132,4},{136,8},{140,12},{144,16},{148,20},{152,24},{156,2... | collective-permute-start | bytes 1179656 | tf_op jit(solution)/shard_map/ppermute | solution.py:17
  42.8 5.2 %collective-permute-start.10 = (bf16[128,1536]{1,0:T(8,128)(2,1)}, bf16[128,1536]{1,0:T(8,128)(2,1)S(1)}, u32[]{:S(2)}, u32[]{:S(2)}) collective-permute-start(bf16[128,1536]{1,0:T(8,128)(2,1)} %pad_maximum_fusion), channel_id=1, source_target_pairs={{0,128},{4,132},{8,136},{12,140},{16,144},{20,148},{24,152},{28,15... | collective-permute-start | bytes 1179656 | tf_op jit(solution)/shard_map/ppermute | solution.py:17
  48.0 2.8 %collective-permute-start.9 = (bf16[128,1536]{1,0:T(8,128)(2,1)}, bf16[128,1536]{1,0:T(8,128)(2,1)S(1)}, u32[]{:S(2)}, u32[]{:S(2)}) collective-permute-start(bf16[128,1536]{1,0:T(8,128)(2,1)} %pad_maximum_fusion), channel_id=1, source_target_pairs={{64,0},{68,4},{72,8},{76,12},{80,16},{84,20},{88,24},{92,28},{96,3... | collective-permute-start | bytes 1179656 | tf_op jit(solution)/shard_map/ppermute | solution.py:17
  52.5 3.0 %collective-permute-start.8 = (bf16[128,1536]{1,0:T(8,128)(2,1)}, bf16[128,1536]{1,0:T(8,128)(2,1)}, u32[]{:S(2)}, u32[]{:S(2)}) collective-permute-start(bf16[128,1536]{1,0:T(8,128)(2,1)} %pad_maximum_fusion), channel_id=1, source_target_pairs={{0,64},{4,68},{8,72},{12,76},{16,80},{20,84},{24,88},{28,92},{32,9... | collective-permute-start | bytes 1179656 | tf_op jit(solution)/shard_map/ppermute | solution.py:17
  56.5 10.0 %collective-permute-start.6 = (bf16[128,1536]{1,0:T(8,128)(2,1)}, bf16[128,1536]{1,0:T(8,128)(2,1)}, u32[]{:S(2)}, u32[]{:S(2)}) collective-permute-start(bf16[128,1536]{1,0:T(8,128)(2,1)} %pad_maximum_fusion), channel_id=1, source_target_pairs={{0,32},{4,36},{8,40},{12,44},{16,48},{20,52},{24,56},{28,60},{32,6... | collective-permute-start | bytes 1179656 | tf_op jit(solution)/shard_map/ppermute | solution.py:17
  67.8 3.7 %collective-permute-start.5 = (bf16[128,1536]{1,0:T(8,128)(2,1)}, bf16[128,1536]{1,0:T(8,128)(2,1)}, u32[]{:S(2)}, u32[]{:S(2)}) collective-permute-start(bf16[128,1536]{1,0:T(8,128)(2,1)} %pad_maximum_fusion), channel_id=1, source_target_pairs={{16,0},{20,4},{24,8},{28,12},{32,16},{36,20},{40,24},{44,28},{48,3... | collective-permute-start | bytes 1179656 | tf_op jit(solution)/shard_map/ppermute | solution.py:17
  72.6 3.1 %collective-permute-start.4 = (bf16[128,1536]{1,0:T(8,128)(2,1)}, bf16[128,1536]{1,0:T(8,128)(2,1)}, u32[]{:S(2)}, u32[]{:S(2)}) collective-permute-start(bf16[128,1536]{1,0:T(8,128)(2,1)} %pad_maximum_fusion), channel_id=1, source_target_pairs={{0,16},{4,20},{8,24},{12,28},{16,32},{20,36},{24,40},{28,44},{32,4... | collective-permute-start | bytes 1179656 | tf_op jit(solution)/shard_map/ppermute | solution.py:17
  75.9 2.5 %collective-permute-start.3 = (bf16[128,1536]{1,0:T(8,128)(2,1)}, bf16[128,1536]{1,0:T(8,128)(2,1)}, u32[]{:S(2)}, u32[]{:S(2)}) collective-permute-start(bf16[128,1536]{1,0:T(8,128)(2,1)} %pad_maximum_fusion), channel_id=1, source_target_pairs={{8,0},{12,4},{16,8},{20,12},{24,16},{28,20},{32,24},{36,28},{40,32... | collective-permute-start | bytes 1179656 | tf_op jit(solution)/shard_map/ppermute | solution.py:17
  78.6 4.1 %collective-permute-start.2 = (bf16[128,1536]{1,0:T(8,128)(2,1)}, bf16[128,1536]{1,0:T(8,128)(2,1)}, u32[]{:S(2)}, u32[]{:S(2)}) collective-permute-start(bf16[128,1536]{1,0:T(8,128)(2,1)} %pad_maximum_fusion), channel_id=1, source_target_pairs={{0,8},{4,12},{8,16},{12,20},{16,24},{20,28},{24,32},{28,36},{32,40... | collective-permute-start | bytes 1179656 | tf_op jit(solution)/shard_map/ppermute | solution.py:17
  84.6 34.8 %collective-permute-done.6 = bf16[128,1536]{1,0:T(8,128)(2,1)} collective-permute-done((bf16[128,1536]{1,0:T(8,128)(2,1)}, bf16[128,1536]{1,0:T(8,128)(2,1)}, u32[]{:S(2)}, u32[]{:S(2)}) %collective-permute-start.6) | collective-permute-done | bytes 393248 | tf_op jit(solution)/shard_map/ppermute | solution.py:17
  119.4 14.4 %collective-permute-start.7 = (bf16[128,1536]{1,0:T(8,128)(2,1)}, bf16[128,1536]{1,0:T(8,128)(2,1)}, u32[]{:S(2)}, u32[]{:S(2)}) collective-permute-start(bf16[128,1536]{1,0:T(8,128)(2,1)} %pad_maximum_fusion), channel_id=1, source_target_pairs={{32,0},{36,4},{40,8},{44,12},{48,16},{52,20},{56,24},{60,28},{64,3... | collective-permute-start | bytes 1179656 | tf_op jit(solution)/shard_map/ppermute | solution.py:17
  135.7 1.8 fusion.160
  138.6 1.8 fusion.161
  142.1 1.8 fusion.162
  145.7 1.8 fusion.163
  180.5 10.9 %all_to_all.70 = bf16[4,32,768]{2,1,0:T(8,128)(2,1)S(1)} all-to-all(bf16[4,32,768]{2,1,0:T(8,128)(2,1)S(1)} %convert_element_type.73), channel_id=1, replica_groups=mesh['ctx'=128,'head'=4] {'head'}, dimensions={0} | all-to-all | bytes 393216 | tf_op jit(solution)/shard_map/all_to_all | solution.py:90
  (157 shorter events, 54.1 us)
Async XLA Ops:
  1.6 7.2 %copy-start.22 = (bf16[32,3072]{1,0:T(8,128)(2,1)S(1)}, bf16[32,3072]{1,0:T(8,128)(2,1)}, u32[]{:S(2)}) copy-start(bf16[32,3072]{1,0:T(8,128)(2,1)} %param.7) | copy-start | bytes 589828
  1.6 14.7 %all-to-all-start.2 = ((bf16[32,4,768]{2,0,1:T(8,128)(2,1)}), bf16[32,4,768]{2,0,1:T(8,128)(2,1)S(1)}, u32[]{:S(2)}, u32[]{:S(2)}) async-start(bf16[32,4,768]{2,0,1:T(8,128)(2,1)} %bitcast.212), calls=%async_computation.2 | async-start | bytes 393216 | tf_op jit(solution)/shard_map/all_to_all | solution.py:36
  6.9 1.3 copy-start.28
  8.9 1.0 copy-start.23
  16.3 35.3 %copy-start.24 = (pred[128,128]{0,1:T(8,128)(4,1)}, pred[128,128]{0,1:T(8,128)(4,1)S(1)}, u32[]{:S(2)}) copy-start(pred[128,128]{0,1:T(8,128)(4,1)S(1)} %get-tuple-element.72) | copy-start | bytes 49156
  16.3 11.1 %all-to-all-start.1 = ((bf16[32,4,768]{2,0,1:T(8,128)(2,1)}), bf16[32,4,768]{2,0,1:T(8,128)(2,1)S(1)}, u32[]{:S(2)}, u32[]{:S(2)}) async-start(bf16[32,4,768]{2,0,1:T(8,128)(2,1)} %bitcast.213), calls=%async_computation.1 | async-start | bytes 393216 | tf_op jit(solution)/shard_map/all_to_all | solution.py:35
  27.4 23.4 %all-to-all-start = ((bf16[32,4,768]{2,0,1:T(8,128)(2,1)}), bf16[32,4,768]{2,0,1:T(8,128)(2,1)S(1)}, u32[]{:S(2)}, u32[]{:S(2)}) async-start(bf16[32,4,768]{2,0,1:T(8,128)(2,1)} %bitcast.214), calls=%async_computation | async-start | bytes 393216 | tf_op jit(solution)/shard_map/all_to_all | solution.py:34
  31.6 20.9 %collective-permute-start.1 = (bf16[128,1536]{1,0:T(8,128)(2,1)}, bf16[128,1536]{1,0:T(8,128)(2,1)S(1)}, u32[]{:S(2)}, u32[]{:S(2)}) collective-permute-start(bf16[128,1536]{1,0:T(8,128)(2,1)} %pad_maximum_fusion), channel_id=1, source_target_pairs={{4,0},{8,4},{12,8},{16,12},{20,16},{24,20},{28,24},{32,28},{36,32}... | collective-permute-start | bytes 1179656 | tf_op jit(solution)/shard_map/ppermute | solution.py:17
  38.1 17.6 %collective-permute-start = (bf16[128,1536]{1,0:T(8,128)(2,1)}, bf16[128,1536]{1,0:T(8,128)(2,1)S(1)}, u32[]{:S(2)}, u32[]{:S(2)}) collective-permute-start(bf16[128,1536]{1,0:T(8,128)(2,1)} %pad_maximum_fusion), channel_id=1, source_target_pairs={{0,4},{4,8},{8,12},{12,16},{16,20},{20,24},{24,28},{28,32},{32,36}... | collective-permute-start | bytes 1179656 | tf_op jit(solution)/shard_map/ppermute | solution.py:17
  40.5 27.2 %collective-permute-start.11 = (bf16[128,1536]{1,0:T(8,128)(2,1)}, bf16[128,1536]{1,0:T(8,128)(2,1)}, u32[]{:S(2)}, u32[]{:S(2)}) collective-permute-start(bf16[128,1536]{1,0:T(8,128)(2,1)} %pad_maximum_fusion), channel_id=1, source_target_pairs={{128,0},{132,4},{136,8},{140,12},{144,16},{148,20},{152,24},{156,2... | collective-permute-start | bytes 1179656 | tf_op jit(solution)/shard_map/ppermute | solution.py:17
  42.8 29.9 %collective-permute-start.10 = (bf16[128,1536]{1,0:T(8,128)(2,1)}, bf16[128,1536]{1,0:T(8,128)(2,1)S(1)}, u32[]{:S(2)}, u32[]{:S(2)}) collective-permute-start(bf16[128,1536]{1,0:T(8,128)(2,1)} %pad_maximum_fusion), channel_id=1, source_target_pairs={{0,128},{4,132},{8,136},{12,140},{16,144},{20,148},{24,152},{28,15... | collective-permute-start | bytes 1179656 | tf_op jit(solution)/shard_map/ppermute | solution.py:17
  48.0 27.9 %collective-permute-start.9 = (bf16[128,1536]{1,0:T(8,128)(2,1)}, bf16[128,1536]{1,0:T(8,128)(2,1)S(1)}, u32[]{:S(2)}, u32[]{:S(2)}) collective-permute-start(bf16[128,1536]{1,0:T(8,128)(2,1)} %pad_maximum_fusion), channel_id=1, source_target_pairs={{64,0},{68,4},{72,8},{76,12},{80,16},{84,20},{88,24},{92,28},{96,3... | collective-permute-start | bytes 1179656 | tf_op jit(solution)/shard_map/ppermute | solution.py:17
  52.5 26.1 %collective-permute-start.8 = (bf16[128,1536]{1,0:T(8,128)(2,1)}, bf16[128,1536]{1,0:T(8,128)(2,1)}, u32[]{:S(2)}, u32[]{:S(2)}) collective-permute-start(bf16[128,1536]{1,0:T(8,128)(2,1)} %pad_maximum_fusion), channel_id=1, source_target_pairs={{0,64},{4,68},{8,72},{12,76},{16,80},{20,84},{24,88},{28,92},{32,9... | collective-permute-start | bytes 1179656 | tf_op jit(solution)/shard_map/ppermute | solution.py:17
  56.5 62.9 %collective-permute-start.6 = (bf16[128,1536]{1,0:T(8,128)(2,1)}, bf16[128,1536]{1,0:T(8,128)(2,1)}, u32[]{:S(2)}, u32[]{:S(2)}) collective-permute-start(bf16[128,1536]{1,0:T(8,128)(2,1)} %pad_maximum_fusion), channel_id=1, source_target_pairs={{0,32},{4,36},{8,40},{12,44},{16,48},{20,52},{24,56},{28,60},{32,6... | collective-permute-start | bytes 1179656 | tf_op jit(solution)/shard_map/ppermute | solution.py:17
  67.8 67.9 %collective-permute-start.5 = (bf16[128,1536]{1,0:T(8,128)(2,1)}, bf16[128,1536]{1,0:T(8,128)(2,1)}, u32[]{:S(2)}, u32[]{:S(2)}) collective-permute-start(bf16[128,1536]{1,0:T(8,128)(2,1)} %pad_maximum_fusion), channel_id=1, source_target_pairs={{16,0},{20,4},{24,8},{28,12},{32,16},{36,20},{40,24},{44,28},{48,3... | collective-permute-start | bytes 1179656 | tf_op jit(solution)/shard_map/ppermute | solution.py:17
  72.6 65.9 %collective-permute-start.4 = (bf16[128,1536]{1,0:T(8,128)(2,1)}, bf16[128,1536]{1,0:T(8,128)(2,1)}, u32[]{:S(2)}, u32[]{:S(2)}) collective-permute-start(bf16[128,1536]{1,0:T(8,128)(2,1)} %pad_maximum_fusion), channel_id=1, source_target_pairs={{0,16},{4,20},{8,24},{12,28},{16,32},{20,36},{24,40},{28,44},{32,4... | collective-permute-start | bytes 1179656 | tf_op jit(solution)/shard_map/ppermute | solution.py:17
  75.9 66.2 %collective-permute-start.3 = (bf16[128,1536]{1,0:T(8,128)(2,1)}, bf16[128,1536]{1,0:T(8,128)(2,1)}, u32[]{:S(2)}, u32[]{:S(2)}) collective-permute-start(bf16[128,1536]{1,0:T(8,128)(2,1)} %pad_maximum_fusion), channel_id=1, source_target_pairs={{8,0},{12,4},{16,8},{20,12},{24,16},{28,20},{32,24},{36,28},{40,32... | collective-permute-start | bytes 1179656 | tf_op jit(solution)/shard_map/ppermute | solution.py:17
  78.6 67.0 %collective-permute-start.2 = (bf16[128,1536]{1,0:T(8,128)(2,1)}, bf16[128,1536]{1,0:T(8,128)(2,1)}, u32[]{:S(2)}, u32[]{:S(2)}) collective-permute-start(bf16[128,1536]{1,0:T(8,128)(2,1)} %pad_maximum_fusion), channel_id=1, source_target_pairs={{0,8},{4,12},{8,16},{12,20},{16,24},{20,28},{24,32},{28,36},{32,40... | collective-permute-start | bytes 1179656 | tf_op jit(solution)/shard_map/ppermute | solution.py:17
  119.4 29.8 %collective-permute-start.7 = (bf16[128,1536]{1,0:T(8,128)(2,1)}, bf16[128,1536]{1,0:T(8,128)(2,1)}, u32[]{:S(2)}, u32[]{:S(2)}) collective-permute-start(bf16[128,1536]{1,0:T(8,128)(2,1)} %pad_maximum_fusion), channel_id=1, source_target_pairs={{32,0},{36,4},{40,8},{44,12},{48,16},{52,20},{56,24},{60,28},{64,3... | collective-permute-start | bytes 1179656 | tf_op jit(solution)/shard_map/ppermute | solution.py:17
  154.4 1.8 copy-start.8
  164.6 0.9 copy-start
  165.5 0.9 copy-start.20
  166.4 0.9 copy-start.2
  174.9 0.9 copy-start.13
  (22 other events, 19.1 us)
where the time goes:
time: 194 us; the launch traced here: 192 us
  starting transfers between devices  67.9 us (35%)
  local copies, waits for them, and re-layouts  51.3 us (26%)
  waiting for transfers between devices  41.1 us (21%)
  other arithmetic  12.3 us (6%)
  blocking collectives  10.9 us (6%)
  matrix products  8.03 us (4%)
    ppermute x12, starting transfers between devices, shifted(): return lax.ppermute(block, axis, route)  55.3 us
    ppermute x12, waiting for transfers between devices, shifted(): return lax.ppermute(block, axis, route)  34.8 us
    slice x24, local copies, waits for them, and re-layouts, on_device(): entries[position][0][:, feature_count:].reshape(row_count, head_count, HD)  23.4 us
    unnamed x62, local copies, waits for them, and re-layouts  12.6 us
    all_to_all x1, blocking collectives, on_device(): lax.all_to_all(result, 'head', split_axis=0, concat_axis=1, tiled=True)  10.9 us
    and x2, other arithmetic, masked_scores(): block_rule(band_index, band_offsets, band_widths, block_mask, row_count)  10.4 us
    slice x12, local copies, waits for them, and re-layouts, masked_scores(): paired_keys[:, :feature_count].reshape(row_count, head_count, HD)  9.13 us
    all_to_all x1, waiting for transfers between devices, on_device(): lax.all_to_all(keys, 'head', split_axis=1, concat_axis=0, tiled=True)  6.32 us
  transfers between devices with their start and end apart: 15, of which 2 were waited for; matrix products, arithmetic and copies ran while one was open for 19% of the time, Pallas kernels for 0%

commit v1 on v0

v1 whole, which is shorter than its diff:
```python
import functools
import math

import jax
import jax.numpy as jnp
from jax import lax
from jax.experimental import pallas as pl
from jax.experimental.pallas import tpu as pltpu
from jax.sharding import PartitionSpec as P

HD = 128
BLOCKS = 8
NBANDS = 7
HEADS = 3
COLS = HEADS * HD
SCALE = HD ** (-0.5) * math.log2(math.e)
NEG = -1e30
MESH = pl.DeviceIdType.MESH


def place(f):
    f = lax.rem(f + 128, 128)
    return lax.rem(f, 4), lax.div(f, 16), lax.rem(lax.div(f, 4), 2), lax.rem(lax.div(f, 8), 2)


def kernel(
    q_ref, k_ref, v_ref, offset_ref, width_ref, mask_ref, out_ref,
    own, query, xbuf, ybuf, mate, bias, top, total, acc, stage,
    own_sem, query_sem, x_sem, y_sem, mate_sem, out_sem, a2a_send, flow_send, out_send,
):
    ctx, x = lax.axis_index("ctx"), lax.axis_index("head")
    y, z, core = lax.div(ctx, 16), lax.rem(lax.div(ctx, 2), 8), lax.rem(ctx, 2)

    def at(y_, z_, core_):
        return (y_ * 8 + z_) * 2 + core_

    frames = [16 * y + x + 4 * core + 8 * s for s in range(2)]
    home_x, _, home_core, home_slot = place(ctx)
    at_home = (home_x == x) & (home_core == core)
    mate_id = (at(y, z, 1 - core), x)
    up_id = (at(lax.rem(y + 1, 8), z, core), x)
    down_id = (at(lax.rem(y + 7, 8), z, core), x)

    def neighbour(s, step):
        nx, ny, ncore, nslot = place(frames[s] + step)
        return (at(ny, z, ncore), nx), nslot

    after = [neighbour(s, 1) for s in range(2)]
    before = [neighbour(s, -1) for s in range(2)]

    barrier = pltpu.get_barrier_semaphore()

    def greet(device):
        pl.semaphore_signal(barrier, inc=1, device_id=device, device_id_type=MESH)

    def home_of(dz):
        g = lax.rem(z + dz, 8)
        return (at(y, g, home_core), home_x), g

    for device in [mate_id, up_id, down_id] + [n for n, _ in after + before]:
        greet(device)
    for dz in range(1, 8):
        greet(home_of(dz)[0])
    for dt in range(1, 4):
        for s in range(2):
            greet((frames[s], lax.rem(x + dt, 4)))

    @pl.when(jnp.logical_not(at_home))
    def _():
        greet(home_of(0)[0])

    for s in range(2):
        @pl.when(frames[s] != ctx)
        def _():
            greet((frames[s], x))

    pl.semaphore_wait(barrier, 23 - 2 * at_home.astype(jnp.int32))

    token_rows = pl.ds(pl.multiple_of(x * 32, 32), 32)

    def spread(src, dst, recv, send, dz):
        device, _ = home_of(dz)
        if dz:
            pltpu.make_async_remote_copy(
                src_ref=src, dst_ref=dst, send_sem=a2a_send.at[send], recv_sem=recv,
                device_id=device, device_id_type=MESH,
            ).start()
        else:
            @pl.when(at_home)
            def _():
                pltpu.make_async_copy(src, dst, recv).start()

            @pl.when(jnp.logical_not(at_home))
            def _():
                pltpu.make_async_remote_copy(
                    src_ref=src, dst_ref=dst, send_sem=a2a_send.at[3 + send], recv_sem=recv,
                    device_id=device, device_id_type=MESH,
                ).start()

    def spread_head(h):
        for dz in (4, 3, 5, 2, 6, 1, 7, 0):
            g = lax.rem(z + dz, 8)
            columns = pl.ds(pl.multiple_of(g * COLS + h * HD, HD), HD)
            for n, ref in ((0, k_ref), (1, v_ref)):
                spread(ref.at[:, columns], own.at[h, home_slot, n, token_rows], own_sem.at[h], n, dz)

    def spread_queries():
        for dz in (4, 3, 5, 2, 6, 1, 7, 0):
            g = lax.rem(z + dz, 8)
            columns = pl.ds(pl.multiple_of(g * COLS, HD), COLS)
            spread(q_ref.at[:, columns], query.at[home_slot, token_rows], query_sem.at[0], 2, dz)

    def arrived(ref, sem):
        pltpu.make_async_copy(ref, ref, sem).wait()

    def send(src, dst, recv, category, device):
        pltpu.make_async_remote_copy(
            src_ref=src, dst_ref=dst, send_sem=flow_send.at[category], recv_sem=recv,
            device_id=device, device_id_type=MESH,
        ).start()

    def first_sends(h):
        arrived(own.at[h], own_sem.at[h])
        send(own.at[h], ybuf.at[0, h], y_sem.at[0, h], 0, up_id)
        send(own.at[h], ybuf.at[1, h], y_sem.at[1, h], 1, down_id)
        for s in range(2):
            device, slot = after[s]
            send(own.at[h, s], xbuf.at[0, h, slot], x_sem.at[0, h, slot], 2, device)
            device, slot = before[s]
            send(own.at[h, s], xbuf.at[1, h, slot], x_sem.at[1, h, slot], 3, device)
        send(own.at[h], mate.at[h, pl.ds(0, 2)], mate_sem.at[0, h], 4, mate_id)

    def second_sends(h):
        for s in range(2):
            arrived(xbuf.at[0, h, s], x_sem.at[0, h, s])
            device, slot = after[s]
            send(xbuf.at[0, h, s], xbuf.at[2, h, slot], x_sem.at[2, h, slot], 5, device)
            arrived(xbuf.at[1, h, s], x_sem.at[1, h, s])
            device, slot = before[s]
            send(xbuf.at[1, h, s], xbuf.at[3, h, slot], x_sem.at[3, h, slot], 6, device)
        arrived(ybuf.at[0, h], y_sem.at[0, h])
        send(ybuf.at[0, h], ybuf.at[2, h], y_sem.at[2, h], 7, up_id)
        arrived(ybuf.at[1, h], y_sem.at[1, h])
        send(ybuf.at[1, h], ybuf.at[3, h], y_sem.at[3, h], 8, down_id)
        send(ybuf.at[1 - core, h, core], mate.at[h, 2], mate_sem.at[1, h], 9, mate_id)

    for h in range(HEADS):
        spread_head(h)
        if h == 0:
            spread_queries()

    key_block = lax.div(lax.broadcasted_iota(jnp.int32, (HD, HD), 0), 16)
    query_block = lax.div(lax.broadcasted_iota(jnp.int32, (HD, HD), 1), 16)
    distance = key_block - query_block
    for b in range(NBANDS):
        active = jnp.zeros((HD, HD), jnp.int32)
        for block in range(BLOCKS):
            active = jnp.where(query_block == block, mask_ref[b, block], active)
        allowed = (active == 1) & (jnp.abs(distance - offset_ref[b]) < width_ref[b])
        if b == 0:
            allowed = allowed | (distance == 0)
        bias[b] = jnp.where(allowed, 0.0, NEG)
    bias[NBANDS] = jnp.full((HD, HD), NEG, jnp.float32)

    def band(b, s, step):
        source = 16 * y + x + 4 * core + 8 * s + step
        return jnp.where((source >= 0) & (source < 128), b, NBANDS)

    def attend(h, s, sets, first=False):
        q = query[s, :, h * HD : (h + 1) * HD]
        scores = [
            lax.dot_general(ref[0], q, (((1,), (1,)), ((), ())), preferred_element_type=jnp.float32) * SCALE
            + bias[index]
            for ref, index in sets
        ]
        peak = functools.reduce(jnp.maximum, scores).max(axis=0, keepdims=True)
        if not first:
            old = top[h, s]
            peak = jnp.maximum(peak, old)
        weights = [jnp.exp2(score - peak) for score in scores]
        added = functools.reduce(jnp.add, weights).sum(axis=0, keepdims=True)
        summed = [
            lax.dot_general(
                ref[1], weight.astype(jnp.bfloat16), (((0,), (0,)), ((), ())),
                preferred_element_type=jnp.float32,
            )
            for (ref, _), weight in zip(sets, weights)
        ]
        summed = functools.reduce(jnp.add, summed)
        top[h, s] = peak
        if first:
            total[h, s] = added
            acc[h, s] = summed
        else:
            kept = jnp.exp2(old - peak)
            total[h, s] = total[h, s] * kept + added
            acc[h, s] = acc[h, s] * kept + summed

    def both(f):
        for s in range(2):
            f(s)

    def attend_own(h):
        both(lambda s: attend(h, s, [(own.at[h, s], 0), (own.at[h, 1 - s], 4)], first=True))

    def attend_x(h):
        both(lambda s: attend(h, s, [(xbuf.at[0, h, s], band(1, s, -1)), (xbuf.at[1, h, s], band(1, s, 1))]))

    def attend_y(h):
        both(lambda s: attend(h, s, [
            (ybuf.at[0, h, s], band(5, s, -16)),
            (ybuf.at[1, h, s], band(5, s, 16)),
            (ybuf.at[s, h, 1 - s], band(4, s, 8 if s else -8)),
        ]))

    def attend_mate(h):
        arrived(mate.at[h, pl.ds(0, 2)], mate_sem.at[0, h])
        arrived(mate.at[h, 2], mate_sem.at[1, h])
        for s in range(2):
            at_end = core == s
            other = jnp.where(at_end, 2, 1 - s)
            ends = band(3, s, 4 if s else -4)
            attend(h, s, [(mate.at[h, s], 3), (mate.at[h, other], jnp.where(at_end, ends, 3))])

    def attend_x2(h):
        for s in range(2):
            arrived(xbuf.at[2, h, s], x_sem.at[2, h, s])
            arrived(xbuf.at[3, h, s], x_sem.at[3, h, s])
            attend(h, s, [(xbuf.at[2, h, s], band(2, s, -2)), (xbuf.at[3, h, s], band(2, s, 2))])

    def attend_y2(h):
        arrived(ybuf.at[2, h], y_sem.at[2, h])
        arrived(ybuf.at[3, h], y_sem.at[3, h])
        both(lambda s: attend(h, s, [(ybuf.at[2, h, s], band(6, s, -32)), (ybuf.at[3, h, s], band(6, s, 32))]))

    def finish(h):
        columns = pl.ds(pl.multiple_of(z * COLS + h * HD, HD), HD)
        for s in range(2):
            stage[h, s] = (acc[h, s] / total[h, s]).T.astype(jnp.bfloat16)
            for dt in (2, 1, 3, 0):
                t = lax.rem(x + dt, 4)
                src = stage.at[h, s, pl.ds(pl.multiple_of(t * 32, 32), 32)]
                dst = out_ref.at[:, columns]

                def remote(sem):
                    pltpu.make_async_remote_copy(
                        src_ref=src, dst_ref=dst, send_sem=sem, recv_sem=out_sem.at[0],
                        device_id=(frames[s], t), device_id_type=MESH,
                    ).start()

                if dt:
                    remote(out_send.at[2])
                else:
                    @pl.when(frames[s] == ctx)
                    def _():
                        pltpu.make_async_copy(src, dst, out_sem.at[0]).start()

                    @pl.when(frames[s] != ctx)
                    def _():
                        remote(out_send.at[s])

    first_sends(0)
    arrived(query, query_sem.at[0])
    attend_own(0)
    first_sends(1)
    attend_own(1)
    second_sends(0)
    first_sends(2)
    attend_own(2)
    attend_x(0)
    second_sends(1)
    attend_y(0)
    attend_mate(0)
    attend_x(1)
    second_sends(2)
    attend_y(1)
    attend_mate(1)
    attend_x2(0)
    attend_y2(0)
    finish(0)
    attend_x(2)
    attend_y(2)
    attend_mate(2)
    attend_x2(1)
    attend_y2(1)
    finish(1)
    attend_x2(2)
    attend_y2(2)
    finish(2)

    for n, ref in ((0, k_ref), (1, v_ref), (2, q_ref)):
        part = ref.at[:, pl.ds(0, 7 * COLS)]
        arrived(part, a2a_send.at[n])

        @pl.when(jnp.logical_not(at_home))
        def _():
            part = ref.at[:, pl.ds(0, COLS)]
            arrived(part, a2a_send.at[3 + n])

    for category in range(9):
        arrived(own, flow_send.at[category])
    arrived(mate.at[:, 2], flow_send.at[9])
    part = stage.at[:, :, pl.ds(0, 96)]
    arrived(part, out_send.at[2])
    for s in range(2):
        @pl.when(frames[s] != ctx)
        def _():
            part = stage.at[:, s, pl.ds(0, 32)]
            arrived(part, out_send.at[s])
    arrived(out_ref, out_sem.at[0])


def on_device(queries, keys, values, band_offsets, band_widths, block_mask):
    bf16 = jnp.bfloat16
    dma = pltpu.SemaphoreType.DMA
    hbm, smem = pl.BlockSpec(memory_space=pl.ANY), pl.BlockSpec(memory_space=pltpu.SMEM)
    return pl.pallas_call(
        kernel,
        out_shape=jax.ShapeDtypeStruct(queries.shape, bf16),
        in_specs=[hbm] * 3 + [smem] * 3,
        out_specs=hbm,
        scratch_shapes=[
            pltpu.VMEM((HEADS, 2, 2, HD, HD), bf16),
            pltpu.VMEM((2, HD, COLS), bf16),
            pltpu.VMEM((4, HEADS, 2, 2, HD, HD), bf16),
            pltpu.VMEM((4, HEADS, 2, 2, HD, HD), bf16),
            pltpu.VMEM((HEADS, 3, 2, HD, HD), bf16),
            pltpu.VMEM((NBANDS + 1, HD, HD), jnp.float32),
            pltpu.VMEM((HEADS, 2, 1, HD), jnp.float32),
            pltpu.VMEM((HEADS, 2, 1, HD), jnp.float32),
            pltpu.VMEM((HEADS, 2, HD, HD), jnp.float32),
            pltpu.VMEM((HEADS, 2, HD, HD), bf16),
            dma((HEADS,)),
            dma((1,)),
            dma((4, HEADS, 2)),
            dma((4, HEADS)),
            dma((2, HEADS)),
            dma((1,)),
            dma((6,)),
            dma((10,)),
            dma((3,)),
        ],
        compiler_params=pltpu.CompilerParams(
            collective_id=0, has_side_effects=True, vmem_limit_bytes=40 * 2**20
        ),
    )(queries, keys, values, band_offsets, band_widths, block_mask)


def solution(mesh):
    tokens = P(("ctx", "head"), None)
    return jax.shard_map(
        on_device,
        mesh=mesh,
        in_specs=(tokens, tokens, tokens, P(), P(), P()),
        out_specs=tokens,
        check_vma=False,
    )
```

time: 194 us -> 63.3 us (0.33)
  the two profiles are of different devices: /device:TPU:96 before, /device:TPU:1 now
where the time goes in v1:
time: 63.3 us; the launch traced here: 62.2 us
  Pallas kernels  56.7 us (90%)
  local copies, waits for them, and re-layouts  5.45 us (9%)
    pallas_call x1, Pallas kernels, on_device(): pl.pallas_call(kernel, out_shape=jax.ShapeDtypeStruct(queries.shape, bf16...  56.7 us
    unnamed x13, local copies, waits for them, and re-layouts  5.45 us

profile of v1, /device:TPU:1, one launch (start us, length us, event | category | flops | bytes accessed | tf_op | source)
XLA Modules:
  0.0 62.2 jit_solution(5423054444520604286)
XLA Ops:
  0.0 0.0 copy-start
  0.0 0.9 %copy-done = bf16[32,3072]{1,0:T(8,128)(2,1)S(1)} copy-done((bf16[32,3072]{1,0:T(8,128)(2,1)S(1)}, bf16[32,3072]{1,0:T(8,128)(2,1)}, u32[]{:S(2)}) %copy-start) | copy-done | bytes 196632
  0.9 0.0 copy-start.1
  0.9 0.9 %copy-done.1 = bf16[32,3072]{1,0:T(8,128)(2,1)S(1)} copy-done((bf16[32,3072]{1,0:T(8,128)(2,1)S(1)}, bf16[32,3072]{1,0:T(8,128)(2,1)}, u32[]{:S(2)}) %copy-start.1) | copy-done | bytes 196632
  1.9 0.0 copy-start.2
  1.9 0.9 %copy-done.2 = bf16[32,3072]{1,0:T(8,128)(2,1)S(1)} copy-done((bf16[32,3072]{1,0:T(8,128)(2,1)S(1)}, bf16[32,3072]{1,0:T(8,128)(2,1)}, u32[]{:S(2)}) %copy-start.2) | copy-done | bytes 196632
  2.8 0.0 copy-start.3
  2.8 0.7 %copy-done.3 = s32[7,8]{1,0:T(8,128)S(1)} copy-done((s32[7,8]{1,0:T(8,128)S(1)}, s32[7,8]{1,0:T(8,128)}, u32[]{:S(2)}) %copy-start.3) | copy-done | bytes 248
  3.5 0.0 copy-start.4
  3.5 0.7 %copy-done.4 = s32[7]{0:T(128)S(1)} copy-done((s32[7]{0:T(128)S(1)}, s32[7]{0:T(128)}, u32[]{:S(2)}) %copy-start.4) | copy-done | bytes 52
  4.1 0.0 copy-start.5
  4.1 0.7 %copy-done.5 = s32[7]{0:T(128)S(1)} copy-done((s32[7]{0:T(128)S(1)}, s32[7]{0:T(128)}, u32[]{:S(2)}) %copy-start.5) | copy-done | bytes 52
  4.8 56.7 %shard_map.64 = bf16[32,3072]{1,0:T(8,128)(2,1)S(1)} custom-call(bf16[32,3072]{1,0:T(8,128)(2,1)S(1)} %copy-done, bf16[32,3072]{1,0:T(8,128)(2,1)S(1)} %copy-done.1, bf16[32,3072]{1,0:T(8,128)(2,1)S(1)} %copy-done.2, s32[7]{0:T(128)S(1)} %copy-done.4, s32[7]{0:T(128)S(1)} %copy-done.5, s32[7,8]{1,0:T(8,128)S(1)} %copy-done.3), custom_call_target="tpu_custom_call" | custom-call | tf_op jit(solution)/shard_map/pallas_call | solution.py:317
  61.5 0.7 %copy.8 = bf16[32,3072]{1,0:T(8,128)(2,1)} copy(bf16[32,3072]{1,0:T(8,128)(2,1)S(1)} %shard_map.64) | data formatting | bytes 393216
Async XLA Ops:
  0.0 0.9 %copy-start = (bf16[32,3072]{1,0:T(8,128)(2,1)S(1)}, bf16[32,3072]{1,0:T(8,128)(2,1)}, u32[]{:S(2)}) copy-start(bf16[32,3072]{1,0:T(8,128)(2,1)} %q_ref.1) | copy-start | bytes 589828
  0.9 0.9 %copy-start.1 = (bf16[32,3072]{1,0:T(8,128)(2,1)S(1)}, bf16[32,3072]{1,0:T(8,128)(2,1)}, u32[]{:S(2)}) copy-start(bf16[32,3072]{1,0:T(8,128)(2,1)} %k_ref.1) | copy-start | bytes 589828
  1.9 0.9 %copy-start.2 = (bf16[32,3072]{1,0:T(8,128)(2,1)S(1)}, bf16[32,3072]{1,0:T(8,128)(2,1)}, u32[]{:S(2)}) copy-start(bf16[32,3072]{1,0:T(8,128)(2,1)} %v_ref.1) | copy-start | bytes 589828
  2.8 0.7 %copy-start.3 = (s32[7,8]{1,0:T(8,128)S(1)}, s32[7,8]{1,0:T(8,128)}, u32[]{:S(2)}) copy-start(s32[7,8]{1,0:T(8,128)} %mask_ref.1) | copy-start | bytes 676
  3.5 0.7 %copy-start.4 = (s32[7]{0:T(128)S(1)}, s32[7]{0:T(128)}, u32[]{:S(2)}) copy-start(s32[7]{0:T(128)} %offset_ref.1) | copy-start | bytes 88
  4.1 0.7 %copy-start.5 = (s32[7]{0:T(128)S(1)}, s32[7]{0:T(128)}, u32[]{:S(2)}) copy-start(s32[7]{0:T(128)} %width_ref.1) | copy-start | bytes 88

commit v2 on v0

v2 whole, which is shorter than its diff:
```python
import functools
import itertools
import math

import jax
import jax.numpy as jnp
from jax import lax
from jax.experimental import pallas as pl
from jax.experimental.pallas import tpu as pltpu
from jax.sharding import PartitionSpec as P

HD = 128
BLOCKS = 8
NBANDS = 7
HEADS = 3
COLS = HEADS * HD
SCALE = HD ** (-0.5) * math.log2(math.e)
NEG = -1e30
MESH = pl.DeviceIdType.MESH


def place(f):
    f = lax.rem(f + 128, 128)
    return lax.rem(f, 4), lax.div(f, 16), lax.rem(lax.div(f, 4), 2), lax.rem(lax.div(f, 8), 2)


def kernel(
    q_ref, k_ref, v_ref, offset_hbm, width_hbm, mask_hbm, out_ref,
    offset_ref, width_ref, mask_ref, own, query, xbuf, x2buf, ybuf, mate, bias, top, total, acc, stage,
    table_sem, own_sem, query_sem, x_sem, x2_sem, y_sem, mate_sem, out_sem, a2a_send, flow_send, out_send,
):
    tables = [
        pltpu.make_async_copy(src, dst, table_sem.at[n])
        for n, (src, dst) in enumerate(
            [(offset_hbm, offset_ref), (width_hbm, width_ref), (mask_hbm, mask_ref)]
        )
    ]
    for copy in tables:
        copy.start()
    ctx, x = lax.axis_index("ctx"), lax.axis_index("head")
    y, z, core = lax.div(ctx, 16), lax.rem(lax.div(ctx, 2), 8), lax.rem(ctx, 2)

    def at(y_, z_, core_):
        return (y_ * 8 + z_) * 2 + core_

    frames = [16 * y + x + 4 * core + 8 * s for s in range(2)]
    home_x, _, home_core, home_slot = place(ctx)
    at_home = (home_x == x) & (home_core == core)
    mate_id = (at(y, z, 1 - core), x)
    up_id = (at(lax.rem(y + 1, 8), z, core), x)
    down_id = (at(lax.rem(y + 7, 8), z, core), x)

    def neighbours(step):
        ids, slots = [], []
        for s in range(2):
            nx, ny, ncore, nslot = place(frames[s] + step)
            ids.append((at(ny, z, ncore), nx))
            slots.append(nslot)
        return ids, slots, ncore

    after, after_slot, after_core = neighbours(1)
    before, before_slot, before_core = neighbours(-1)

    barrier = pltpu.get_barrier_semaphore()

    def greet(device):
        pl.semaphore_signal(barrier, inc=1, device_id=device, device_id_type=MESH)

    def home_of(dz):
        return (at(y, lax.rem(z + dz, 8), home_core), home_x)

    for device in [mate_id, up_id, down_id] + after + before:
        greet(device)
    for dz in range(1, 8):
        greet(home_of(dz))
    for dt in range(1, 4):
        for s in range(2):
            greet((frames[s], lax.rem(x + dt, 4)))

    @pl.when(jnp.logical_not(at_home))
    def _():
        greet(home_of(0))

    for s in range(2):
        @pl.when(frames[s] != ctx)
        def _():
            greet((frames[s], x))

    relays = x == 1 + core
    takes = x == 3 * core

    @pl.when(takes)
    def _():
        greet((at(y, z, 1 - core), 2 - core))

    pl.semaphore_wait(barrier, 23 - 2 * at_home.astype(jnp.int32) + relays.astype(jnp.int32))

    token_rows = pl.ds(pl.multiple_of(x * 32, 32), 32)

    def spread(h, n):
        ref = (k_ref, v_ref, q_ref)[n]
        if n == 2:
            dst, recv = query.at[h, home_slot, token_rows], query_sem.at[h]
        else:
            dst, recv = own.at[h, n, home_slot, token_rows], own_sem.at[h, n]

        def remote(src, dz, sem):
            pltpu.make_async_remote_copy(
                src_ref=src, dst_ref=dst, send_sem=a2a_send.at[sem], recv_sem=recv,
                device_id=home_of(dz), device_id_type=MESH,
            ).start()

        for dz in (4, 3, 5, 2, 6, 1, 7, 0):
            g = lax.rem(z + dz, 8)
            src = ref.at[:, pl.ds(pl.multiple_of(g * COLS + h * HD, HD), HD)]
            if dz:
                remote(src, dz, n)
            else:
                @pl.when(at_home)
                def _():
                    pltpu.make_async_copy(src, dst, recv).start()

                @pl.when(jnp.logical_not(at_home))
                def _():
                    remote(src, dz, 3 + n)

    def arrived(ref, sem):
        pltpu.make_async_copy(ref, ref, sem).wait()

    def send(src, dst, recv, category, device):
        pltpu.make_async_remote_copy(
            src_ref=src, dst_ref=dst, send_sem=flow_send.at[category], recv_sem=recv,
            device_id=device, device_id_type=MESH,
        ).start()

    def pick(first, pair):
        return tuple(jnp.where(first, p, q) for p, q in zip(*pair))

    to_first = jnp.where(after_slot[0] == 0, 0, 1)
    to_last = jnp.where(before_slot[1] == 1, 1, 0)
    first_id = pick(to_first == 0, after)
    middle_after_id = pick(to_first == 1, after)
    last_id = pick(to_last == 0, before)
    middle_before_id = pick(to_last == 1, before)

    sends_first = jnp.logical_not((x == 3) & (core == 1))
    sends_last = jnp.logical_not((x == 0) & (core == 0))

    def sends_1(h, n):
        arrived(own.at[h, n], own_sem.at[h, n])
        send(own.at[h, n], ybuf.at[0, h, n], y_sem.at[0, h, n], 0, up_id)
        send(own.at[h, n], ybuf.at[1, h, n], y_sem.at[1, h, n], 1, down_id)
        for s in range(2):
            to = after_slot[s]
            send(own.at[h, n, s], xbuf.at[0, h, n, to], x_sem.at[0, h, n, to], 2, after[s])
            to = before_slot[s]
            send(own.at[h, n, s], xbuf.at[1, h, n, to], x_sem.at[1, h, n, to], 3, before[s])
        send(own.at[h, n], mate.at[h, n, pl.ds(0, 2)], mate_sem.at[0, h, n], 4, mate_id)

    def sends_2(h, n):
        arrived(ybuf.at[0, h, n], y_sem.at[0, h, n])
        send(ybuf.at[0, h, n], ybuf.at[2, h, n], y_sem.at[2, h, n], 9, up_id)
        arrived(ybuf.at[1, h, n], y_sem.at[1, h, n])
        send(ybuf.at[1, h, n], ybuf.at[3, h, n], y_sem.at[3, h, n], 10, down_id)
        end = ybuf.at[1 - core, h, n, core]
        send(end, mate.at[h, n, 2], mate_sem.at[1, h, n], 11, mate_id)

        @pl.when(relays)
        def _():
            send(end, x2buf.at[h, n, 1 - core], x2_sem.at[1 - core, h, n], 14, (at(y, z, 1 - core), 3 - 3 * core))

        for d in range(2):
            for s in range(2):
                arrived(xbuf.at[d, h, n, s], x_sem.at[d, h, n, s])

        @pl.when(sends_first)
        def _():
            send(xbuf.at[0, h, n, to_first], x2buf.at[h, n, 0], x2_sem.at[0, h, n], 5, first_id)

        @pl.when(sends_last)
        def _():
            send(xbuf.at[1, h, n, to_last], x2buf.at[h, n, 1], x2_sem.at[1, h, n], 6, last_id)

        if n == 0:
            @pl.when(after_core == 0)
            def _():
                send(xbuf.at[0, h, n, 1 - to_first], x2buf.at[h, n, 2], x2_sem.at[2, h, n], 7, middle_after_id)
        else:
            @pl.when(before_core == 1)
            def _():
                send(xbuf.at[1, h, n, 1 - to_last], x2buf.at[h, n, 2], x2_sem.at[2, h, n], 8, middle_before_id)

    def sends_3(h, n):
        arrived(x2buf.at[h, n, 0], x2_sem.at[0, h, n])
        arrived(x2buf.at[h, n, 1], x2_sem.at[1, h, n])
        send(x2buf.at[h, n, 1 - core], x2buf.at[h, n, 3], x2_sem.at[3, h, n], 12, mate_id)
        arrived_middle = functools.partial(arrived, x2buf.at[h, n, 2], x2_sem.at[2, h, n])

        @pl.when(core == n)
        def _():
            arrived_middle()
            send(x2buf.at[h, n, 2], x2buf.at[h, n, 2], x2_sem.at[2, h, n], 13, mate_id)

    def fill_bias():
        for copy in tables:
            copy.wait()
        key_block = lax.div(lax.broadcasted_iota(jnp.int32, (HD, HD), 0), 16)
        query_block = lax.div(lax.broadcasted_iota(jnp.int32, (HD, HD), 1), 16)
        distance = key_block - query_block
        for b in range(NBANDS):
            active = jnp.zeros((HD, HD), jnp.int32)
            for block in range(BLOCKS):
                active = jnp.where(query_block == block, mask_ref[b, block], active)
            allowed = (active == 1) & (jnp.abs(distance - offset_ref[b]) < width_ref[b])
            if b == 0:
                allowed = allowed | (distance == 0)
            bias[b] = jnp.where(allowed, 0.0, NEG)
        bias[NBANDS] = jnp.full((HD, HD), NEG, jnp.float32)

    def band(b, s, step):
        source = 16 * y + x + 4 * core + 8 * s + step
        return jnp.where((source >= 0) & (source < 128), b, NBANDS)

    def attend(work, first=False):
        scores = []
        for h, s, sets in work:
            keys = jnp.concatenate([keys[...] for keys, _, _ in sets], axis=0)
            score = lax.dot_general(
                keys, query[h, s], (((1,), (1,)), ((), ())), preferred_element_type=jnp.float32
            )
            scores.append([
                score[n * HD : (n + 1) * HD] * SCALE + bias[index] for n, (_, _, index) in enumerate(sets)
            ])
        values = [[values[...] for _, values, _ in sets] for _, _, sets in work]
        peaks = [functools.reduce(jnp.maximum, score).max(axis=0, keepdims=True) for score in scores]
        if not first:
            old = [(top[h, s], total[h, s], acc[h, s]) for h, s, _ in work]
            peaks = [jnp.maximum(peak, before[0]) for peak, before in zip(peaks, old)]
        results = []
        for n, (score, peak) in enumerate(zip(scores, peaks)):
            weights = [jnp.exp2(part - peak) for part in score]
            added = functools.reduce(jnp.add, weights).sum(axis=0, keepdims=True)
            summed = [
                lax.dot_general(
                    value, weight.astype(jnp.bfloat16), (((0,), (0,)), ((), ())),
                    preferred_element_type=jnp.float32,
                )
                for value, weight in zip(values[n], weights)
            ]
            summed = functools.reduce(jnp.add, summed)
            if not first:
                kept = jnp.exp2(old[n][0] - peak)
                added, summed = old[n][1] * kept + added, old[n][2] * kept + summed
            results.append((peak, added, summed))
        for (h, s, _), (peak, added, summed) in zip(work, results):
            top[h, s], total[h, s], acc[h, s] = peak, added, summed

    def entry(ref, where, index):
        return ref.at[where(0)], ref.at[where(1)], index

    def sets_own(h, s):
        return [entry(own, lambda n: (h, n, s), 0), entry(own, lambda n: (h, n, 1 - s), 4)]

    def sets_x(h, s):
        return [
            entry(xbuf, lambda n: (0, h, n, s), band(1, s, -1)),
            entry(xbuf, lambda n: (1, h, n, s), band(1, s, 1)),
        ]

    def sets_y(h, s):
        return [
            entry(ybuf, lambda n: (0, h, n, s), band(5, s, -16)),
            entry(ybuf, lambda n: (1, h, n, s), band(5, s, 16)),
            entry(ybuf, lambda n: (s, h, n, 1 - s), band(4, s, 8 if s else -8)),
        ]

    def sets_mate(h, s):
        at_end = core == s
        other = jnp.where(at_end, 2, 1 - s)
        ends = band(3, s, 4 if s else -4)
        return [
            entry(mate, lambda n: (h, n, s), 3),
            entry(mate, lambda n: (h, n, other), jnp.where(at_end, ends, 3)),
        ]

    def sets_x2(h, s):
        earlier, later = (0, 3 - core) if s == 0 else (2 + core, 1)
        return [
            entry(x2buf, lambda n: (h, n, earlier), band(2, s, -2)),
            entry(x2buf, lambda n: (h, n, later), band(2, s, 2)),
        ]

    def sets_y2(h, s):
        return [
            entry(ybuf, lambda n: (2, h, n, s), band(6, s, -32)),
            entry(ybuf, lambda n: (3, h, n, s), band(6, s, 32)),
        ]

    def both(h, *kinds, first=False):
        attend([(h, s, sum((sets(h, s) for sets in kinds), [])) for s in range(2)], first)

    def wait_query(h):
        arrived(query.at[h], query_sem.at[h])

    def wait_mate(h):
        for n in range(2):
            arrived(mate.at[h, n, pl.ds(0, 2)], mate_sem.at[0, h, n])
            arrived(mate.at[h, n, 2], mate_sem.at[1, h, n])

    def wait_x2(h):
        for n in range(2):
            @pl.when(core != n)
            def _():
                arrived(x2buf.at[h, n, 2], x2_sem.at[2, h, n])

            arrived(x2buf.at[h, n, 3], x2_sem.at[3, h, n])

    def wait_y2(h):
        for n in range(2):
            arrived(ybuf.at[2, h, n], y_sem.at[2, h, n])
            arrived(ybuf.at[3, h, n], y_sem.at[3, h, n])

    def finish(h):
        columns = pl.ds(pl.multiple_of(z * COLS + h * HD, HD), HD)
        for s in range(2):
            stage[h, s] = (acc[h, s] / total[h, s]).T.astype(jnp.bfloat16)
        for dt, s in itertools.product((2, 1, 3, 0), range(2)):
            t = lax.rem(x + dt, 4)
            src = stage.at[h, s, pl.ds(pl.multiple_of(t * 32, 32), 32)]
            dst = out_ref.at[:, columns]

            def remote(sem):
                pltpu.make_async_remote_copy(
                    src_ref=src, dst_ref=dst, send_sem=sem, recv_sem=out_sem.at[0],
                    device_id=(frames[s], t), device_id_type=MESH,
                ).start()

            if dt:
                remote(out_send.at[2])
            else:
                @pl.when(frames[s] == ctx)
                def _():
                    pltpu.make_async_copy(src, dst, out_sem.at[0]).start()

                @pl.when(frames[s] != ctx)
                def _():
                    remote(out_send.at[s])

    K, V, Q = 0, 1, 2
    for h, n in ((0, K), (0, V), (1, K), (1, V), (0, Q), (2, K), (2, V), (1, Q), (2, Q)):
        spread(h, n)
    fill_bias()
    sends_1(0, K)
    sends_1(0, V)
    sends_1(1, K)
    sends_2(0, K)
    sends_1(1, V)
    sends_2(0, V)
    sends_1(2, K)
    sends_2(1, K)
    sends_1(2, V)
    sends_2(1, V)
    sends_3(0, K)
    sends_3(0, V)
    wait_query(0)
    both(0, sets_own, sets_x, sets_y, first=True)
    sends_2(2, K)
    sends_3(1, K)
    wait_mate(0)
    wait_x2(0)
    both(0, sets_mate, sets_x2)
    wait_query(1)
    both(1, sets_own, sets_x, sets_y, first=True)
    sends_2(2, V)
    sends_3(1, V)
    wait_y2(0)
    both(0, sets_y2)
    finish(0)
    wait_query(2)
    both(2, sets_own, sets_x, sets_y, first=True)
    wait_mate(1)
    wait_x2(1)
    wait_y2(1)
    both(1, sets_mate, sets_x2, sets_y2)
    finish(1)
    sends_3(2, K)
    sends_3(2, V)
    wait_mate(2)
    wait_x2(2)
    both(2, sets_mate, sets_x2)
    wait_y2(2)
    both(2, sets_y2)
    finish(2)

    for n, ref in ((0, k_ref), (1, v_ref), (2, q_ref)):
        part = ref.at[:, pl.ds(0, 7 * COLS)]
        arrived(part, a2a_send.at[n])

        @pl.when(jnp.logical_not(at_home))
        def _():
            part = ref.at[:, pl.ds(0, COLS)]
            arrived(part, a2a_send.at[3 + n])

    half, sixth = own.at[:, :, 0], own.at[:, 0, 0]
    for category in (0, 1, 2, 3, 4, 9, 10):
        arrived(own, flow_send.at[category])
    for category in (11, 12):
        arrived(half, flow_send.at[category])
    for category, sent in ((5, sends_first), (6, sends_last), (14, relays)):
        @pl.when(sent)
        def _():
            arrived(half, flow_send.at[category])

    arrived(sixth, flow_send.at[13])

    @pl.when(after_core == 0)
    def _():
        arrived(sixth, flow_send.at[7])

    @pl.when(before_core == 1)
    def _():
        arrived(sixth, flow_send.at[8])

    part = stage.at[:, :, pl.ds(0, 96)]
    arrived(part, out_send.at[2])
    for s in range(2):
        @pl.when(frames[s] != ctx)
        def _():
            part = stage.at[:, s, pl.ds(0, 32)]
            arrived(part, out_send.at[s])
    arrived(out_ref, out_sem.at[0])


def on_device(queries, keys, values, band_offsets, band_widths, block_mask):
    bf16 = jnp.bfloat16
    dma = pltpu.SemaphoreType.DMA
    hbm = pl.BlockSpec(memory_space=pl.ANY)
    return pl.pallas_call(
        kernel,
        out_shape=jax.ShapeDtypeStruct(queries.shape, bf16),
        in_specs=[hbm] * 6,
        out_specs=hbm,
        scratch_shapes=[
            pltpu.SMEM(band_offsets.shape, jnp.int32),
            pltpu.SMEM(band_widths.shape, jnp.int32),
            pltpu.SMEM(block_mask.shape, jnp.int32),
            pltpu.VMEM((HEADS, 2, 2, HD, HD), bf16),
            pltpu.VMEM((HEADS, 2, HD, HD), bf16),
            pltpu.VMEM((2, HEADS, 2, 2, HD, HD), bf16),
            pltpu.VMEM((HEADS, 2, 4, HD, HD), bf16),
            pltpu.VMEM((4, HEADS, 2, 2, HD, HD), bf16),
            pltpu.VMEM((HEADS, 2, 3, HD, HD), bf16),
            pltpu.VMEM((NBANDS + 1, HD, HD), jnp.float32),
            pltpu.VMEM((HEADS, 2, 1, HD), jnp.float32),
            pltpu.VMEM((HEADS, 2, 1, HD), jnp.float32),
            pltpu.VMEM((HEADS, 2, HD, HD), jnp.float32),
            pltpu.VMEM((HEADS, 2, HD, HD), bf16),
            dma((3,)),
            dma((HEADS, 2)),
            dma((HEADS,)),
            dma((2, HEADS, 2, 2)),
            dma((4, HEADS, 2)),
            dma((4, HEADS, 2)),
            dma((2, HEADS, 2)),
            dma((1,)),
            dma((6,)),
            dma((15,)),
            dma((3,)),
        ],
        compiler_params=pltpu.CompilerParams(
            collective_id=0, has_side_effects=True, vmem_limit_bytes=60 * 2**20
        ),
    )(queries, keys, values, band_offsets, band_widths, block_mask)


def solution(mesh):
    tokens = P(("ctx", "head"), None)
    return jax.shard_map(
        on_device,
        mesh=mesh,
        in_specs=(tokens, tokens, tokens, P(), P(), P()),
        out_specs=tokens,
        check_vma=False,
    )
```

time: 194 us -> 53.5 us (0.28)
  the two profiles are of different devices: /device:TPU:96 before, /device:TPU:1 now
where the time goes in v2:
time: 53.5 us; the launch traced here: 53.4 us
  Pallas kernels  51.8 us (97%)
  local copies, waits for them, and re-layouts  1.62 us (3%)
    pallas_call x1, Pallas kernels, on_device(): pl.pallas_call(kernel, out_shape=jax.ShapeDtypeStruct(queries.shape, bf16...  51.8 us
    unnamed x1, local copies, waits for them, and re-layouts  1.62 us

profile of v2, /device:TPU:1, one launch (start us, length us, event | category | flops | bytes accessed | tf_op | source)
XLA Modules:
  0.0 53.4 jit_solution(6866821582639851985)
XLA Ops:
  0.0 51.8 %shard_map.64 = bf16[32,3072]{1,0:T(8,128)(2,1)} custom-call(bf16[32,3072]{1,0:T(8,128)(2,1)} %q_ref.1, bf16[32,3072]{1,0:T(8,128)(2,1)} %k_ref.1, bf16[32,3072]{1,0:T(8,128)(2,1)} %v_ref.1, s32[7]{0:T(128)} %offset_hbm.1, s32[7]{0:T(128)} %width_hbm.1, s32[7,8]{1,0:T(8,128)} %mask_hbm.1), custom_call_target="tpu_custom_call" | custom-call | tf_op jit(solution)/shard_map/pallas_call | solution.py:438
  51.8 1.6 %copy.8 = bf16[32,3072]{1,0:T(8,128)(2,1)} copy(bf16[32,3072]{1,0:T(8,128)(2,1)} %shard_map.64) | data formatting | bytes 393216

commit v3 on v2

--- a/solution.py
+++ b/solution.py
@@ -26,9 +26,67 @@
 
 def kernel(
     q_ref, k_ref, v_ref, offset_hbm, width_hbm, mask_hbm, out_ref,
-    offset_ref, width_ref, mask_ref, own, query, xbuf, x2buf, ybuf, mate, bias, top, total, acc, stage,
-    table_sem, own_sem, query_sem, x_sem, x2_sem, y_sem, mate_sem, out_sem, a2a_send, flow_send, out_send,
+    offset_ref, width_ref, mask_ref, own, query, xbuf, x2buf, ybuf, y2buf, mate, bias, top, total, acc, stage,
+    table_sem, own_sem, query_sem, x_sem, x2_sem, middle_sem, pair_sem, y_sem, y2_sem, mate_sem, out_sem,
+    a2a_send, flow_send, out_send,
 ):
+    ctx, x = lax.axis_index("ctx"), lax.axis_index("head")
+    y, z, core = lax.div(ctx, 16), lax.rem(lax.div(ctx, 2), 8), lax.rem(ctx, 2)
+
+    def at(y_, z_, core_):
+        return (y_ * 8 + z_) * 2 + core_
+
+    frames = [16 * y + x + 4 * core + 8 * s for s in range(2)]
+    home_x, _, home_core, home_slot = place(ctx)
+    at_home = (home_x == x) & (home_core == core)
+    mate_id = (at(y, z, 1 - core), x)
+    up_id = (at(lax.rem(y + 1, 8), z, core), x)
+    down_id = (at(lax.rem(y + 7, 8), z, core), x)
+
+    def neighbours(step):
+        ids, slots = [], []
+        for s in range(2):
+            nx, ny, ncore, nslot = place(frames[s] + step)
+            ids.append((at(ny, z, ncore), nx))
+            slots.append(nslot)
+        return ids, slots, ncore
+
+    after, after_slot, after_core = neighbours(1)
+    before, before_slot, before_core = neighbours(-1)
+
+    barrier = pltpu.get_barrier_semaphore()
+
+    def greet(device):
+        pl.semaphore_signal(barrier, inc=1, device_id=device, device_id_type=MESH)
+
+    def home_of(dz):
+        return (at(y, lax.rem(z + dz, 8), home_core), home_x)
+
+    for dz in (4, 3, 5, 2, 6, 1, 7):
+        greet(home_of(dz))
+    for dt in range(1, 4):
+        for s in range(2):
+            greet((frames[s], lax.rem(x + dt, 4)))
+
+    @pl.when(jnp.logical_not(at_home))
+    def _():
+        greet(home_of(0))
+
+    for s in range(2):
+        @pl.when(frames[s] != ctx)
+        def _():
+            greet((frames[s], x))
+
+    relays = x == 1 + core
+    takes = x == 3 * core
+
+    for device in [mate_id, up_id, down_id] + after + before:
+        greet(device)
+
+    @pl.when(takes)
+    def _():
+        greet((at(y, z, 1 - core), 2 - core))
+
     tables = [
         pltpu.make_async_copy(src, dst, table_sem.at[n])
         for n, (src, dst) in enumerate(
@@ -37,62 +95,6 @@
     ]
     for copy in tables:
         copy.start()
-    ctx, x = lax.axis_index("ctx"), lax.axis_index("head")
-    y, z, core = lax.div(ctx, 16), lax.rem(lax.div(ctx, 2), 8), lax.rem(ctx, 2)
-
-    def at(y_, z_, core_):
-        return (y_ * 8 + z_) * 2 + core_
-
-    frames = [16 * y + x + 4 * core + 8 * s for s in range(2)]
-    home_x, _, home_core, home_slot = place(ctx)
-    at_home = (home_x == x) & (home_core == core)
-    mate_id = (at(y, z, 1 - core), x)
-    up_id = (at(lax.rem(y + 1, 8), z, core), x)
-    down_id = (at(lax.rem(y + 7, 8), z, core), x)
-
-    def neighbours(step):
-        ids, slots = [], []
-        for s in range(2):
-            nx, ny, ncore, nslot = place(frames[s] + step)
-            ids.append((at(ny, z, ncore), nx))
-            slots.append(nslot)
-        return ids, slots, ncore
-
-    after, after_slot, after_core = neighbours(1)
-    before, before_slot, before_core = neighbours(-1)
-
-    barrier = pltpu.get_barrier_semaphore()
-
-    def greet(device):
-        pl.semaphore_signal(barrier, inc=1, device_id=device, device_id_type=MESH)
-
-    def home_of(dz):
-        return (at(y, lax.rem(z + dz, 8), home_core), home_x)
-
-    for device in [mate_id, up_id, down_id] + after + before:
-        greet(device)
-    for dz in range(1, 8):
-        greet(home_of(dz))
-    for dt in range(1, 4):
-        for s in range(2):
-            greet((frames[s], lax.rem(x + dt, 4)))
-
-    @pl.when(jnp.logical_not(at_home))
-    def _():
-        greet(home_of(0))
-
-    for s in range(2):
-        @pl.when(frames[s] != ctx)
-        def _():
-            greet((frames[s], x))
-
-    relays = x == 1 + core
-    takes = x == 3 * core
-
-    @pl.when(takes)
-    def _():
-        greet((at(y, z, 1 - core), 2 - core))
-
     pl.semaphore_wait(barrier, 23 - 2 * at_home.astype(jnp.int32) + relays.astype(jnp.int32))
 
     token_rows = pl.ds(pl.multiple_of(x * 32, 32), 32)
@@ -122,7 +124,7 @@
 
                 @pl.when(jnp.logical_not(at_home))
                 def _():
-                    remote(src, dz, 3 + n)
+                    remote(src, dz, 3)
 
     def arrived(ref, sem):
         pltpu.make_async_copy(ref, ref, sem).wait()
@@ -143,63 +145,78 @@
     last_id = pick(to_last == 0, before)
     middle_before_id = pick(to_last == 1, before)
 
+    inner, inmost = (y > 0) & (y < 7), (y > 1) & (y < 6)
+    zeros = jnp.zeros((HEADS, 2, 2, HD, HD), jnp.bfloat16)
+    for ref, d, missing in ((ybuf, 0, y < 1), (ybuf, 1, y > 6), (y2buf, 0, y < 2), (y2buf, 1, y > 5)):
+        @pl.when(missing)
+        def _():
+            ref[:, :, d] = zeros
+
     sends_first = jnp.logical_not((x == 3) & (core == 1))
     sends_last = jnp.logical_not((x == 0) & (core == 0))
 
     def sends_1(h, n):
         arrived(own.at[h, n], own_sem.at[h, n])
-        send(own.at[h, n], ybuf.at[0, h, n], y_sem.at[0, h, n], 0, up_id)
-        send(own.at[h, n], ybuf.at[1, h, n], y_sem.at[1, h, n], 1, down_id)
+
+        @pl.when(y < 7)
+        def _():
+            send(own.at[h, n], ybuf.at[h, n, 0], y_sem.at[h, n], 0, up_id)
+
+        @pl.when(y > 0)
+        def _():
+            send(own.at[h, n], ybuf.at[h, n, 1], y_sem.at[h, n], 0, down_id)
+
         for s in range(2):
-            to = after_slot[s]
-            send(own.at[h, n, s], xbuf.at[0, h, n, to], x_sem.at[0, h, n, to], 2, after[s])
-            to = before_slot[s]
-            send(own.at[h, n, s], xbuf.at[1, h, n, to], x_sem.at[1, h, n, to], 3, before[s])
-        send(own.at[h, n], mate.at[h, n, pl.ds(0, 2)], mate_sem.at[0, h, n], 4, mate_id)
-
-    def sends_2(h, n):
-        arrived(ybuf.at[0, h, n], y_sem.at[0, h, n])
-        send(ybuf.at[0, h, n], ybuf.at[2, h, n], y_sem.at[2, h, n], 9, up_id)
-        arrived(ybuf.at[1, h, n], y_sem.at[1, h, n])
-        send(ybuf.at[1, h, n], ybuf.at[3, h, n], y_sem.at[3, h, n], 10, down_id)
-        end = ybuf.at[1 - core, h, n, core]
-        send(end, mate.at[h, n, 2], mate_sem.at[1, h, n], 11, mate_id)
+            send(own.at[h, n, s], xbuf.at[h, n, 0, after_slot[s]], x_sem.at[h, n], 2, after[s])
+            send(own.at[h, n, s], xbuf.at[h, n, 1, before_slot[s]], x_sem.at[h, n], 2, before[s])
+        send(own.at[h, n], mate.at[h, n, pl.ds(0, 2)], mate_sem.at[h], 3, mate_id)
+
+    def sends_2y(h, n):
+        @pl.when(inner)
+        def _():
+            arrived(ybuf.at[h, n], y_sem.at[h, n])
+            send(ybuf.at[h, n, 0], y2buf.at[h, n, 0], y2_sem.at[h], 1, up_id)
+            send(ybuf.at[h, n, 1], y2buf.at[h, n, 1], y2_sem.at[h], 1, down_id)
+
+        @pl.when(jnp.logical_not(inner))
+        def _():
+            arrived(ybuf.at[h, n, 0], y_sem.at[h, n])
+
+        end = ybuf.at[h, n, 1 - core, core]
+        send(end, mate.at[h, n, 2], mate_sem.at[h], 3, mate_id)
 
         @pl.when(relays)
         def _():
-            send(end, x2buf.at[h, n, 1 - core], x2_sem.at[1 - core, h, n], 14, (at(y, z, 1 - core), 3 - 3 * core))
-
-        for d in range(2):
-            for s in range(2):
-                arrived(xbuf.at[d, h, n, s], x_sem.at[d, h, n, s])
+            send(end, x2buf.at[h, n, 1 - core], x2_sem.at[h, n], 9, (at(y, z, 1 - core), 3 - 3 * core))
+
+    def sends_2x(h, n):
+        arrived(xbuf.at[h, n], x_sem.at[h, n])
 
         @pl.when(sends_first)
         def _():
-            send(xbuf.at[0, h, n, to_first], x2buf.at[h, n, 0], x2_sem.at[0, h, n], 5, first_id)
+            send(xbuf.at[h, n, 0, to_first], x2buf.at[h, n, 0], x2_sem.at[h, n], 5, first_id)
 
         @pl.when(sends_last)
         def _():
-            send(xbuf.at[1, h, n, to_last], x2buf.at[h, n, 1], x2_sem.at[1, h, n], 6, last_id)
+            send(xbuf.at[h, n, 1, to_last], x2buf.at[h, n, 1], x2_sem.at[h, n], 6, last_id)
 
         if n == 0:
             @pl.when(after_core == 0)
             def _():
-                send(xbuf.at[0, h, n, 1 - to_first], x2buf.at[h, n, 2], x2_sem.at[2, h, n], 7, middle_after_id)
+                send(xbuf.at[h, n, 0, 1 - to_first], x2buf.at[h, n, 2], middle_sem.at[h], 7, middle_after_id)
         else:
             @pl.when(before_core == 1)
             def _():
-                send(xbuf.at[1, h, n, 1 - to_last], x2buf.at[h, n, 2], x2_sem.at[2, h, n], 8, middle_before_id)
+                send(xbuf.at[h, n, 1, 1 - to_last], x2buf.at[h, n, 2], middle_sem.at[h], 8, middle_before_id)
 
     def sends_3(h, n):
-        arrived(x2buf.at[h, n, 0], x2_sem.at[0, h, n])
-        arrived(x2buf.at[h, n, 1], x2_sem.at[1, h, n])
-        send(x2buf.at[h, n, 1 - core], x2buf.at[h, n, 3], x2_sem.at[3, h, n], 12, mate_id)
-        arrived_middle = functools.partial(arrived, x2buf.at[h, n, 2], x2_sem.at[2, h, n])
+        arrived(x2buf.at[h, n, pl.ds(0, 2)], x2_sem.at[h, n])
+        send(x2buf.at[h, n, 1 - core], x2buf.at[h, n, 3], pair_sem.at[h], 4, mate_id)
 
         @pl.when(core == n)
         def _():
-            arrived_middle()
-            send(x2buf.at[h, n, 2], x2buf.at[h, n, 2], x2_sem.at[2, h, n], 13, mate_id)
+            arrived(x2buf.at[h, n, 2], middle_sem.at[h])
+            send(x2buf.at[h, n, 2], x2buf.at[h, n, 2], pair_sem.at[h], 4, mate_id)
 
     def fill_bias():
         for copy in tables:
@@ -263,15 +280,15 @@
 
     def sets_x(h, s):
         return [
-            entry(xbuf, lambda n: (0, h, n, s), band(1, s, -1)),
-            entry(xbuf, lambda n: (1, h, n, s), band(1, s, 1)),
+            entry(xbuf, lambda n: (h, n, 0, s), band(1, s, -1)),
+            entry(xbuf, lambda n: (h, n, 1, s), band(1, s, 1)),
         ]
 
     def sets_y(h, s):
         return [
-            entry(ybuf, lambda n: (0, h, n, s), band(5, s, -16)),
-            entry(ybuf, lambda n: (1, h, n, s), band(5, s, 16)),
-            entry(ybuf, lambda n: (s, h, n, 1 - s), band(4, s, 8 if s else -8)),
+            entry(ybuf, lambda n: (h, n, 0, s), band(5, s, -16)),
+            entry(ybuf, lambda n: (h, n, 1, s), band(5, s, 16)),
+            entry(ybuf, lambda n: (h, n, s, 1 - s), band(4, s, 8 if s else -8)),
         ]
 
     def sets_mate(h, s):
@@ -292,8 +309,8 @@
 
     def sets_y2(h, s):
         return [
-            entry(ybuf, lambda n: (2, h, n, s), band(6, s, -32)),
-            entry(ybuf, lambda n: (3, h, n, s), band(6, s, 32)),
+            entry(y2buf, lambda n: (h, n, 0, s), band(6, s, -32)),
+            entry(y2buf, lambda n: (h, n, 1, s), band(6, s, 32)),
         ]
 
     def both(h, *kinds, first=False):
@@ -303,22 +320,19 @@
         arrived(query.at[h], query_sem.at[h])
 
     def wait_mate(h):
-        for n in range(2):
-            arrived(mate.at[h, n, pl.ds(0, 2)], mate_sem.at[0, h, n])
-            arrived(mate.at[h, n, 2], mate_sem.at[1, h, n])
+        arrived(mate.at[h], mate_sem.at[h])
 
     def wait_x2(h):
-        for n in range(2):
-            @pl.when(core != n)
-            def _():
-                arrived(x2buf.at[h, n, 2], x2_sem.at[2, h, n])
-
-            arrived(x2buf.at[h, n, 3], x2_sem.at[3, h, n])
+        arrived(x2buf.at[h, 0, pl.ds(0, 3)], pair_sem.at[h])
 
     def wait_y2(h):
-        for n in range(2):
-            arrived(ybuf.at[2, h, n], y_sem.at[2, h, n])
-            arrived(ybuf.at[3, h, n], y_sem.at[3, h, n])
+        @pl.when(inmost)
+        def _():
+            arrived(y2buf.at[h], y2_sem.at[h])
+
+        @pl.when(jnp.logical_not(inmost))
+        def _():
+            arrived(y2buf.at[h, :, 0], y2_sem.at[h])
 
     def finish(h):
         columns = pl.ds(pl.multiple_of(z * COLS + h * HD, HD), HD)
@@ -347,31 +361,37 @@
                     remote(out_send.at[s])
 
     K, V, Q = 0, 1, 2
-    for h, n in ((0, K), (0, V), (1, K), (1, V), (0, Q), (2, K), (2, V), (1, Q), (2, Q)):
+    for h, n in ((0, K), (0, V), (1, K), (1, V), (2, K), (2, V), (0, Q), (1, Q), (2, Q)):
         spread(h, n)
     fill_bias()
     sends_1(0, K)
     sends_1(0, V)
     sends_1(1, K)
-    sends_2(0, K)
+    sends_2y(0, K)
+    sends_2x(0, K)
     sends_1(1, V)
-    sends_2(0, V)
+    sends_2y(0, V)
+    sends_2x(0, V)
     sends_1(2, K)
-    sends_2(1, K)
+    sends_2y(1, K)
+    sends_2x(1, K)
     sends_1(2, V)
-    sends_2(1, V)
+    sends_2y(1, V)
+    sends_2x(1, V)
     sends_3(0, K)
     sends_3(0, V)
     wait_query(0)
     both(0, sets_own, sets_x, sets_y, first=True)
-    sends_2(2, K)
+    sends_2y(2, K)
+    sends_2x(2, K)
     sends_3(1, K)
     wait_mate(0)
     wait_x2(0)
     both(0, sets_mate, sets_x2)
     wait_query(1)
     both(1, sets_own, sets_x, sets_y, first=True)
-    sends_2(2, V)
+    sends_2y(2, V)
+    sends_2x(2, V)
     sends_3(1, V)
     wait_y2(0)
     both(0, sets_y2)
@@ -386,40 +406,36 @@
     sends_3(2, K)
     sends_3(2, V)
     wait_mate(2)
+    wait_y2(2)
+    both(2, sets_mate, sets_y2)
     wait_x2(2)
-    both(2, sets_mate, sets_x2)
-    wait_y2(2)
-    both(2, sets_y2)
+    both(2, sets_x2)
     finish(2)
 
     for n, ref in ((0, k_ref), (1, v_ref), (2, q_ref)):
         part = ref.at[:, pl.ds(0, 7 * COLS)]
         arrived(part, a2a_send.at[n])
 
-        @pl.when(jnp.logical_not(at_home))
-        def _():
-            part = ref.at[:, pl.ds(0, COLS)]
-            arrived(part, a2a_send.at[3 + n])
-
-    half, sixth = own.at[:, :, 0], own.at[:, 0, 0]
-    for category in (0, 1, 2, 3, 4, 9, 10):
-        arrived(own, flow_send.at[category])
-    for category in (11, 12):
-        arrived(half, flow_send.at[category])
-    for category, sent in ((5, sends_first), (6, sends_last), (14, relays)):
+    @pl.when(jnp.logical_not(at_home))
+    def _():
+        part = q_ref.at[:, pl.ds(0, 3 * COLS)]
+        arrived(part, a2a_send.at[3])
+
+    for category, ref in ((2, xbuf), (3, mate), (4, x2buf.at[:, 0, pl.ds(0, 3)])):
+        arrived(ref, flow_send.at[category])
+    for category, ref, sent in (
+        (0, ybuf, inner),
+        (0, ybuf.at[:, :, 0], jnp.logical_not(inner)),
+        (1, y2buf, inner),
+        (5, x2buf.at[:, :, 0], sends_first),
+        (6, x2buf.at[:, :, 0], sends_last),
+        (7, x2buf.at[:, 0, 0], after_core == 0),
+        (8, x2buf.at[:, 0, 0], before_core == 1),
+        (9, x2buf.at[:, :, 0], relays),
+    ):
         @pl.when(sent)
         def _():
-            arrived(half, flow_send.at[category])
-
-    arrived(sixth, flow_send.at[13])
-
-    @pl.when(after_core == 0)
-    def _():
-        arrived(sixth, flow_send.at[7])
-
-    @pl.when(before_core == 1)
-    def _():
-        arrived(sixth, flow_send.at[8])
+            arrived(ref, flow_send.at[category])
 
     part = stage.at[:, :, pl.ds(0, 96)]
     arrived(part, out_send.at[2])
@@ -446,9 +462,10 @@
             pltpu.SMEM(block_mask.shape, jnp.int32),
             pltpu.VMEM((HEADS, 2, 2, HD, HD), bf16),
             pltpu.VMEM((HEADS, 2, HD, HD), bf16),
-            pltpu.VMEM((2, HEADS, 2, 2, HD, HD), bf16),
+            pltpu.VMEM((HEADS, 2, 2, 2, HD, HD), bf16),
             pltpu.VMEM((HEADS, 2, 4, HD, HD), bf16),
-            pltpu.VMEM((4, HEADS, 2, 2, HD, HD), bf16),
+            pltpu.VMEM((HEADS, 2, 2, 2, HD, HD), bf16),
+            pltpu.VMEM((HEADS, 2, 2, 2, HD, HD), bf16),
             pltpu.VMEM((HEADS, 2, 3, HD, HD), bf16),
             pltpu.VMEM((NBANDS + 1, HD, HD), jnp.float32),
             pltpu.VMEM((HEADS, 2, 1, HD), jnp.float32),
@@ -458,13 +475,16 @@
             dma((3,)),
             dma((HEADS, 2)),
             dma((HEADS,)),
-            dma((2, HEADS, 2, 2)),
-            dma((4, HEADS, 2)),
-            dma((4, HEADS, 2)),
-            dma((2, HEADS, 2)),
+            dma((HEADS, 2)),
+            dma((HEADS, 2)),
+            dma((HEADS,)),
+            dma((HEADS,)),
+            dma((HEADS, 2)),
+            dma((HEADS,)),
+            dma((HEADS,)),
             dma((1,)),
-            dma((6,)),
-            dma((15,)),
+            dma((4,)),
+            dma((10,)),
             dma((3,)),
         ],
         compiler_params=pltpu.CompilerParams(

time: 53.5 us -> 50.4 us (0.942); the launches traced: 53.4 us -> 49.7 us
  Pallas kernels: 51.8 us -> 48.1 us
    pallas_call x1, Pallas kernels: 51.8 us -> 48.1 us  [on_device(): pl.pallas_call(kernel, out_shape=jax.ShapeDtypeStruct(queries.shape, bf16...]
where the time goes in v3:
time: 50.4 us; the launch traced here: 49.7 us
  Pallas kernels  48.1 us (95%)
  local copies, waits for them, and re-layouts  1.62 us (3%)
    pallas_call x1, Pallas kernels, on_device(): pl.pallas_call(kernel, out_shape=jax.ShapeDtypeStruct(queries.shape, bf16...  48.1 us
    unnamed x1, local copies, waits for them, and re-layouts  1.62 us

profile of v3, /device:TPU:1, one launch (start us, length us, event | category | flops | bytes accessed | tf_op | source)
XLA Modules:
  0.0 49.7 jit_solution(8592798515777274944)
XLA Ops:
  0.0 48.1 %shard_map.64 = bf16[32,3072]{1,0:T(8,128)(2,1)} custom-call(bf16[32,3072]{1,0:T(8,128)(2,1)} %q_ref.1, bf16[32,3072]{1,0:T(8,128)(2,1)} %k_ref.1, bf16[32,3072]{1,0:T(8,128)(2,1)} %v_ref.1, s32[7]{0:T(128)} %offset_hbm.1, s32[7]{0:T(128)} %width_hbm.1, s32[7,8]{1,0:T(8,128)} %mask_hbm.1), custom_call_target="tpu_custom_call" | custom-call | tf_op jit(solution)/shard_map/pallas_call | solution.py:454
  48.1 1.6 %copy.8 = bf16[32,3072]{1,0:T(8,128)(2,1)} copy(bf16[32,3072]{1,0:T(8,128)(2,1)} %shard_map.64) | data formatting | bytes 393216

commit v4 on v3

--- a/solution.py
+++ b/solution.py
@@ -1,5 +1,4 @@
 import functools
-import itertools
 import math
 
 import jax
@@ -27,7 +26,7 @@
 def kernel(
     q_ref, k_ref, v_ref, offset_hbm, width_hbm, mask_hbm, out_ref,
     offset_ref, width_ref, mask_ref, own, query, xbuf, x2buf, ybuf, y2buf, mate, bias, top, total, acc, stage,
-    table_sem, own_sem, query_sem, x_sem, x2_sem, middle_sem, pair_sem, y_sem, y2_sem, mate_sem, out_sem,
+    table_sem, own_sem, query_sem, x_sem, x2_sem, pair_sem, y_sem, y2_sem, mate_sem, out_sem,
     a2a_send, flow_send, out_send,
 ):
     ctx, x = lax.axis_index("ctx"), lax.axis_index("head")
@@ -36,9 +35,14 @@
     def at(y_, z_, core_):
         return (y_ * 8 + z_) * 2 + core_
 
-    frames = [16 * y + x + 4 * core + 8 * s for s in range(2)]
-    home_x, _, home_core, home_slot = place(ctx)
-    at_home = (home_x == x) & (home_core == core)
+    own_class = lax.rem(x + 8 - z, 4)
+    frames = [16 * y + own_class + 4 * core + 8 * s for s in range(2)]
+    home_class, _, home_core, home_slot = place(ctx)
+    at_home = (home_class == own_class) & (home_core == core)
+
+    def chip(class_, z_):
+        return lax.rem(class_ + z_, 4)
+
     mate_id = (at(y, z, 1 - core), x)
     up_id = (at(lax.rem(y + 1, 8), z, core), x)
     down_id = (at(lax.rem(y + 7, 8), z, core), x)
@@ -46,8 +50,8 @@
     def neighbours(step):
         ids, slots = [], []
         for s in range(2):
-            nx, ny, ncore, nslot = place(frames[s] + step)
-            ids.append((at(ny, z, ncore), nx))
+            nclass, ny, ncore, nslot = place(frames[s] + step)
+            ids.append((at(ny, z, ncore), chip(nclass, z)))
             slots.append(nslot)
         return ids, slots, ncore
 
@@ -60,7 +64,8 @@
         pl.semaphore_signal(barrier, inc=1, device_id=device, device_id_type=MESH)
 
     def home_of(dz):
-        return (at(y, lax.rem(z + dz, 8), home_core), home_x)
+        g = lax.rem(z + dz, 8)
+        return (at(y, g, home_core), chip(home_class, g))
 
     for dz in (4, 3, 5, 2, 6, 1, 7):
         greet(home_of(dz))
@@ -77,15 +82,20 @@
         def _():
             greet((frames[s], x))
 
-    relays = x == 1 + core
-    takes = x == 3 * core
+    relays = own_class == 1 + core
+    takes = own_class == 3 * core
 
     for device in [mate_id, up_id, down_id] + after + before:
         greet(device)
 
+    @pl.when(core == 0)
+    def _():
+        class_, y_, core_, _ = place(frames[0] + 3)
+        greet((at(y_, z, core_), chip(class_, z)))
+
     @pl.when(takes)
     def _():
-        greet((at(y, z, 1 - core), 2 - core))
+        greet((at(y, z, 1 - core), chip(2 - core, z)))
 
     tables = [
         pltpu.make_async_copy(src, dst, table_sem.at[n])
@@ -95,7 +105,7 @@
     ]
     for copy in tables:
         copy.start()
-    pl.semaphore_wait(barrier, 23 - 2 * at_home.astype(jnp.int32) + relays.astype(jnp.int32))
+    pl.semaphore_wait(barrier, 23 - 2 * at_home.astype(jnp.int32) + relays.astype(jnp.int32) + after_core)
 
     token_rows = pl.ds(pl.multiple_of(x * 32, 32), 32)
 
@@ -140,23 +150,26 @@
 
     to_first = jnp.where(after_slot[0] == 0, 0, 1)
     to_last = jnp.where(before_slot[1] == 1, 1, 0)
-    first_id = pick(to_first == 0, after)
-    middle_after_id = pick(to_first == 1, after)
+    first_id, second_id = pick(to_first == 0, after), pick(to_first == 1, after)
+    first_mate_id = (first_id[0] - after_core, first_id[1])
     last_id = pick(to_last == 0, before)
-    middle_before_id = pick(to_last == 1, before)
+    middle_id = pick(to_last == 1, before)
 
     inner, inmost = (y > 0) & (y < 7), (y > 1) & (y < 6)
-    zeros = jnp.zeros((HEADS, 2, 2, HD, HD), jnp.bfloat16)
     for ref, d, missing in ((ybuf, 0, y < 1), (ybuf, 1, y > 6), (y2buf, 0, y < 2), (y2buf, 1, y > 5)):
         @pl.when(missing)
         def _():
-            ref[:, :, d] = zeros
-
-    sends_first = jnp.logical_not((x == 3) & (core == 1))
-    sends_last = jnp.logical_not((x == 0) & (core == 0))
-
-    def sends_1(h, n):
+            part = ref.at[:, :, d] if ref is ybuf else ref.at[:, :, :, d]
+            part[...] = jnp.zeros(part.shape, jnp.bfloat16)
+
+    sends_first = jnp.logical_not((own_class == 3) & (core == 1))
+    sends_last = jnp.logical_not((own_class == 0) & (core == 0))
+    relay_id = (at(y, z, 1 - core), chip(3 - 3 * core, z))
+
+    def sends_1a(h, n):
         arrived(own.at[h, n], own_sem.at[h, n])
+        send(own.at[h, n, to_first], xbuf.at[h, n, 0, 0], x_sem.at[h, n, 0], 2, first_id)
+        send(own.at[h, n, 1 - to_last], xbuf.at[h, n, 0, 1], x_sem.at[h, n, 0], 2, middle_id)
 
         @pl.when(y < 7)
         def _():
@@ -166,57 +179,85 @@
         def _():
             send(own.at[h, n], ybuf.at[h, n, 1], y_sem.at[h, n], 0, down_id)
 
-        for s in range(2):
-            send(own.at[h, n, s], xbuf.at[h, n, 0, after_slot[s]], x_sem.at[h, n], 2, after[s])
-            send(own.at[h, n, s], xbuf.at[h, n, 1, before_slot[s]], x_sem.at[h, n], 2, before[s])
         send(own.at[h, n], mate.at[h, n, pl.ds(0, 2)], mate_sem.at[h], 3, mate_id)
 
-    def sends_2y(h, n):
+    def sends_1b(h, n):
+        send(own.at[h, n, 1 - to_first], xbuf.at[h, n, 1, 0], x_sem.at[h, n, 1], 2, second_id)
+        send(own.at[h, n, to_last], xbuf.at[h, n, 1, 1], x_sem.at[h, n, 1], 2, last_id)
+
+    def send_y2(h, n, s):
         @pl.when(inner)
         def _():
+            send(ybuf.at[h, n, 0, s], y2buf.at[h, s, n, 0], y2_sem.at[h, s], 1, up_id)
+            send(ybuf.at[h, n, 1, s], y2buf.at[h, s, n, 1], y2_sem.at[h, s], 1, down_id)
+
+    def sends_2a(h, n):
+        @pl.when(inner)
+        def _():
             arrived(ybuf.at[h, n], y_sem.at[h, n])
-            send(ybuf.at[h, n, 0], y2buf.at[h, n, 0], y2_sem.at[h], 1, up_id)
-            send(ybuf.at[h, n, 1], y2buf.at[h, n, 1], y2_sem.at[h], 1, down_id)
 
         @pl.when(jnp.logical_not(inner))
         def _():
             arrived(ybuf.at[h, n, 0], y_sem.at[h, n])
 
         end = ybuf.at[h, n, 1 - core, core]
+
+        @pl.when(relays)
+        def _():
+            send(end, x2buf.at[h, n, 1 - core], x2_sem.at[h, n, 1 - core], 8, relay_id)
+
+        send_y2(h, n, 0)
         send(end, mate.at[h, n, 2], mate_sem.at[h], 3, mate_id)
-
-        @pl.when(relays)
-        def _():
-            send(end, x2buf.at[h, n, 1 - core], x2_sem.at[h, n], 9, (at(y, z, 1 - core), 3 - 3 * core))
-
-    def sends_2x(h, n):
-        arrived(xbuf.at[h, n], x_sem.at[h, n])
-
-        @pl.when(sends_first)
-        def _():
-            send(xbuf.at[h, n, 0, to_first], x2buf.at[h, n, 0], x2_sem.at[h, n], 5, first_id)
+        arrived(xbuf.at[h, n, 0], x_sem.at[h, n, 0])
+
+        @pl.when(sends_first & (after_core == 0))
+        def _():
+            send(xbuf.at[h, n, 0, 0], x2buf.at[h, n, 0], x2_sem.at[h, n, 0], 5, first_id)
+
+        @pl.when(after_core == 1)
+        def _():
+            send(xbuf.at[h, n, 0, 0], x2buf.at[h, n, 3], pair_sem.at[h, 0], 5, first_mate_id)
+
+        @pl.when((before_core == 1) & (to_last == 1))
+        def _():
+            send(xbuf.at[h, n, 0, 1], x2buf.at[h, n, 2], pair_sem.at[h, 0], 7, middle_id)
+
+    def sends_2b(h, n):
+        arrived(xbuf.at[h, n, 1], x_sem.at[h, n, 1])
 
         @pl.when(sends_last)
         def _():
-            send(xbuf.at[h, n, 1, to_last], x2buf.at[h, n, 1], x2_sem.at[h, n], 6, last_id)
-
-        if n == 0:
-            @pl.when(after_core == 0)
-            def _():
-                send(xbuf.at[h, n, 0, 1 - to_first], x2buf.at[h, n, 2], middle_sem.at[h], 7, middle_after_id)
-        else:
-            @pl.when(before_core == 1)
-            def _():
-                send(xbuf.at[h, n, 1, 1 - to_last], x2buf.at[h, n, 2], middle_sem.at[h], 8, middle_before_id)
-
-    def sends_3(h, n):
-        arrived(x2buf.at[h, n, pl.ds(0, 2)], x2_sem.at[h, n])
-        send(x2buf.at[h, n, 1 - core], x2buf.at[h, n, 3], pair_sem.at[h], 4, mate_id)
-
-        @pl.when(core == n)
-        def _():
-            arrived(x2buf.at[h, n, 2], middle_sem.at[h])
-            send(x2buf.at[h, n, 2], x2buf.at[h, n, 2], pair_sem.at[h], 4, mate_id)
+            send(xbuf.at[h, n, 1, 1], x2buf.at[h, n, 1], x2_sem.at[h, n, 1], 6, last_id)
+
+        @pl.when((before_core == 1) & (to_last == 0))
+        def _():
+            send(xbuf.at[h, n, 1, 1], x2buf.at[h, n, 2], pair_sem.at[h, 0], 7, middle_id)
+
+    def sends_3b(h, n):
+        arrived(x2buf.at[h, n, 1], x2_sem.at[h, n, 1])
+
+        @pl.when(core == 0)
+        def _():
+            send(x2buf.at[h, n, 1], x2buf.at[h, n, 3], pair_sem.at[h, 1], 4, mate_id)
+
+    def wait_x2a(h):
+        arrived(x2buf.at[h, :, 2], pair_sem.at[h, 0])
+
+        @pl.when(core == 0)
+        def _():
+            for n in range(2):
+                send(x2buf.at[h, n, 3], x2buf.at[h, n, 0], x2_sem.at[h, n, 0], 4, mate_id)
+
+        @pl.when(core == 1)
+        def _():
+            for n in range(2):
+                send(x2buf.at[h, n, 2], x2buf.at[h, n, 2], pair_sem.at[h, 1], 4, mate_id)
+
+        for n in range(2):
+            arrived(x2buf.at[h, n, 0], x2_sem.at[h, n, 0])
+
+    def wait_x2b(h):
+        arrived(x2buf.at[h, :, 2], pair_sem.at[h, 1])
 
     def fill_bias():
         for copy in tables:
@@ -235,12 +276,12 @@
         bias[NBANDS] = jnp.full((HD, HD), NEG, jnp.float32)
 
     def band(b, s, step):
-        source = 16 * y + x + 4 * core + 8 * s + step
+        source = frames[s] + step
         return jnp.where((source >= 0) & (source < 128), b, NBANDS)
 
-    def attend(work, first=False):
+    def attend(*work):
         scores = []
-        for h, s, sets in work:
+        for h, s, sets, _ in work:
             keys = jnp.concatenate([keys[...] for keys, _, _ in sets], axis=0)
             score = lax.dot_general(
                 keys, query[h, s], (((1,), (1,)), ((), ())), preferred_element_type=jnp.float32
@@ -248,28 +289,28 @@
             scores.append([
                 score[n * HD : (n + 1) * HD] * SCALE + bias[index] for n, (_, _, index) in enumerate(sets)
             ])
-        values = [[values[...] for _, values, _ in sets] for _, _, sets in work]
-        peaks = [functools.reduce(jnp.maximum, score).max(axis=0, keepdims=True) for score in scores]
-        if not first:
-            old = [(top[h, s], total[h, s], acc[h, s]) for h, s, _ in work]
-            peaks = [jnp.maximum(peak, before[0]) for peak, before in zip(peaks, old)]
+        values = [[values[...] for _, values, _ in sets] for _, _, sets, _ in work]
+        old = [None if first else (top[h, s], total[h, s], acc[h, s]) for h, s, _, first in work]
         results = []
-        for n, (score, peak) in enumerate(zip(scores, peaks)):
+        for score, value, before in zip(scores, values, old):
+            peak = functools.reduce(jnp.maximum, score).max(axis=0, keepdims=True)
+            if before:
+                peak = jnp.maximum(peak, before[0])
             weights = [jnp.exp2(part - peak) for part in score]
             added = functools.reduce(jnp.add, weights).sum(axis=0, keepdims=True)
             summed = [
                 lax.dot_general(
-                    value, weight.astype(jnp.bfloat16), (((0,), (0,)), ((), ())),
+                    part, weight.astype(jnp.bfloat16), (((0,), (0,)), ((), ())),
                     preferred_element_type=jnp.float32,
                 )
-                for value, weight in zip(values[n], weights)
+                for part, weight in zip(value, weights)
             ]
             summed = functools.reduce(jnp.add, summed)
-            if not first:
-                kept = jnp.exp2(old[n][0] - peak)
-                added, summed = old[n][1] * kept + added, old[n][2] * kept + summed
+            if before:
+                kept = jnp.exp2(before[0] - peak)
+                added, summed = before[1] * kept + added, before[2] * kept + summed
             results.append((peak, added, summed))
-        for (h, s, _), (peak, added, summed) in zip(work, results):
+        for (h, s, _, _), (peak, added, summed) in zip(work, results):
             top[h, s], total[h, s], acc[h, s] = peak, added, summed
 
     def entry(ref, where, index):
@@ -280,8 +321,8 @@
 
     def sets_x(h, s):
         return [
-            entry(xbuf, lambda n: (h, n, 0, s), band(1, s, -1)),
-            entry(xbuf, lambda n: (h, n, 1, s), band(1, s, 1)),
+            entry(xbuf, lambda n: (h, n, s, 0), band(1, s, -1)),
+            entry(xbuf, lambda n: (h, n, s, 1), band(1, s, 1)),
         ]
 
     def sets_y(h, s):
@@ -309,12 +350,15 @@
 
     def sets_y2(h, s):
         return [
-            entry(y2buf, lambda n: (h, n, 0, s), band(6, s, -32)),
-            entry(y2buf, lambda n: (h, n, 1, s), band(6, s, 32)),
+            entry(y2buf, lambda n: (h, s, n, 0), band(6, s, -32)),
+            entry(y2buf, lambda n: (h, s, n, 1), band(6, s, 32)),
         ]
 
-    def both(h, *kinds, first=False):
-        attend([(h, s, sum((sets(h, s) for sets in kinds), [])) for s in range(2)], first)
+    def near(s, h, *more):
+        return h, s, sum((sets(h, s) for sets in (sets_own, sets_x, sets_y) + more), []), True
+
+    def far(s, h, *more):
+        return h, s, sum((sets(h, s) for sets in more + (sets_x2, sets_y2)), []), False
 
     def wait_query(h):
         arrived(query.at[h], query_sem.at[h])
@@ -322,23 +366,19 @@
     def wait_mate(h):
         arrived(mate.at[h], mate_sem.at[h])
 
-    def wait_x2(h):
-        arrived(x2buf.at[h, 0, pl.ds(0, 3)], pair_sem.at[h])
-
-    def wait_y2(h):
+    def wait_y2(h, s):
         @pl.when(inmost)
         def _():
-            arrived(y2buf.at[h], y2_sem.at[h])
+            arrived(y2buf.at[h, s], y2_sem.at[h, s])
 
         @pl.when(jnp.logical_not(inmost))
         def _():
-            arrived(y2buf.at[h, :, 0], y2_sem.at[h])
-
-    def finish(h):
+            arrived(y2buf.at[h, s, :, 0], y2_sem.at[h, s])
+
+    def finish(s, h):
         columns = pl.ds(pl.multiple_of(z * COLS + h * HD, HD), HD)
-        for s in range(2):
-            stage[h, s] = (acc[h, s] / total[h, s]).T.astype(jnp.bfloat16)
-        for dt, s in itertools.product((2, 1, 3, 0), range(2)):
+        stage[h, s] = (acc[h, s] / total[h, s]).T.astype(jnp.bfloat16)
+        for dt in (2, 1, 3, 0):
             t = lax.rem(x + dt, 4)
             src = stage.at[h, s, pl.ds(pl.multiple_of(t * 32, 32), 32)]
             dst = out_ref.at[:, columns]
@@ -364,53 +404,71 @@
     for h, n in ((0, K), (0, V), (1, K), (1, V), (2, K), (2, V), (0, Q), (1, Q), (2, Q)):
         spread(h, n)
     fill_bias()
-    sends_1(0, K)
-    sends_1(0, V)
-    sends_1(1, K)
-    sends_2y(0, K)
-    sends_2x(0, K)
-    sends_1(1, V)
-    sends_2y(0, V)
-    sends_2x(0, V)
-    sends_1(2, K)
-    sends_2y(1, K)
-    sends_2x(1, K)
-    sends_1(2, V)
-    sends_2y(1, V)
-    sends_2x(1, V)
-    sends_3(0, K)
-    sends_3(0, V)
+    sends_1a(0, K)
+    sends_1a(0, V)
+    sends_1a(1, K)
+    sends_2a(0, K)
+    sends_1b(0, K)
+    sends_1a(1, V)
+    sends_2a(0, V)
+    sends_1b(0, V)
+    sends_1a(2, K)
+    sends_2a(1, K)
+    sends_1a(2, V)
+    sends_2a(1, V)
+    sends_1b(1, K)
+    sends_1b(1, V)
+    sends_2b(0, K)
+    sends_2b(0, V)
+    send_y2(0, K, 1)
+    send_y2(0, V, 1)
     wait_query(0)
-    both(0, sets_own, sets_x, sets_y, first=True)
-    sends_2y(2, K)
-    sends_2x(2, K)
-    sends_3(1, K)
+    wait_query(1)
     wait_mate(0)
-    wait_x2(0)
-    both(0, sets_mate, sets_x2)
-    wait_query(1)
-    both(1, sets_own, sets_x, sets_y, first=True)
-    sends_2y(2, V)
-    sends_2x(2, V)
-    sends_3(1, V)
-    wait_y2(0)
-    both(0, sets_y2)
-    finish(0)
+    attend(near(0, 0), near(0, 1), near(1, 0, sets_mate))
+    sends_2a(2, K)
+    sends_1b(2, K)
+    sends_2a(2, V)
+    sends_1b(2, V)
+    for h in (1, 2):
+        send_y2(h, K, 1)
+        send_y2(h, V, 1)
+    sends_2b(1, K)
+    sends_2b(1, V)
+    sends_3b(0, K)
+    sends_3b(0, V)
     wait_query(2)
-    both(2, sets_own, sets_x, sets_y, first=True)
     wait_mate(1)
-    wait_x2(1)
-    wait_y2(1)
-    both(1, sets_mate, sets_x2, sets_y2)
-    finish(1)
-    sends_3(2, K)
-    sends_3(2, V)
+    wait_y2(0, 0)
+    wait_x2a(0)
+    attend(far(0, 0, sets_mate), near(0, 2), near(1, 1, sets_mate))
+    finish(0, 0)
+    wait_y2(1, 0)
+    wait_x2a(1)
+    attend(far(0, 1, sets_mate))
+    finish(0, 1)
+    sends_2b(2, K)
+    sends_2b(2, V)
     wait_mate(2)
-    wait_y2(2)
-    both(2, sets_mate, sets_y2)
-    wait_x2(2)
-    both(2, sets_x2)
-    finish(2)
+    wait_y2(2, 0)
+    wait_x2a(2)
+    attend(far(0, 2, sets_mate))
+    finish(0, 2)
+    sends_3b(1, K)
+    sends_3b(1, V)
+    wait_y2(0, 1)
+    wait_x2b(0)
+    wait_y2(1, 1)
+    wait_x2b(1)
+    attend(far(1, 0), far(1, 1), near(1, 2, sets_mate))
+    finish(1, 0)
+    finish(1, 1)
+    sends_3b(2, K)
+    sends_3b(2, V)
+    wait_y2(2, 1)
+    wait_x2b(2)
+    attend(far(1, 2))
+    finish(1, 2)
 
     for n, ref in ((0, k_ref), (1, v_ref), (2, q_ref)):
         part = ref.at[:, pl.ds(0, 7 * COLS)]
@@ -421,17 +479,18 @@
         part = q_ref.at[:, pl.ds(0, 3 * COLS)]
         arrived(part, a2a_send.at[3])
 
-    for category, ref in ((2, xbuf), (3, mate), (4, x2buf.at[:, 0, pl.ds(0, 3)])):
-        arrived(ref, flow_send.at[category])
+    arrived(xbuf, flow_send.at[2])
+    arrived(mate, flow_send.at[3])
     for category, ref, sent in (
         (0, ybuf, inner),
         (0, ybuf.at[:, :, 0], jnp.logical_not(inner)),
         (1, y2buf, inner),
+        (4, x2buf.at[:, :, pl.ds(0, 2)], core == 0),
+        (4, x2buf.at[:, :, 0], core == 1),
         (5, x2buf.at[:, :, 0], sends_first),
         (6, x2buf.at[:, :, 0], sends_last),
-        (7, x2buf.at[:, 0, 0], after_core == 0),
-        (8, x2buf.at[:, 0, 0], before_core == 1),
-        (9, x2buf.at[:, :, 0], relays),
+        (7, x2buf.at[:, :, 0], before_core == 1),
+        (8, x2buf.at[:, :, 0], relays),
     ):
         @pl.when(sent)
         def _():
@@ -475,16 +534,15 @@
             dma((3,)),
             dma((HEADS, 2)),
             dma((HEADS,)),
+            dma((HEADS, 2, 2)),
+            dma((HEADS, 2, 2)),
+            dma((HEADS, 2)),
             dma((HEADS, 2)),
             dma((HEADS, 2)),
             dma((HEADS,)),
-            dma((HEADS,)),
-            dma((HEADS, 2)),
-            dma((HEADS,)),
-            dma((HEADS,)),
             dma((1,)),
             dma((4,)),
-            dma((10,)),
+            dma((9,)),
             dma((3,)),
         ],
         compiler_params=pltpu.CompilerParams(

time: 50.4 us -> 48.8 us (0.968)
  Pallas kernels: 48.1 us -> 47 us
    pallas_call x1, Pallas kernels: 48.1 us -> 47 us  [on_device(): pl.pallas_call(kernel, out_shape=jax.ShapeDtypeStruct(queries.shape, bf16...]
where the time goes in v4:
time: 48.8 us; the launch traced here: 48.6 us
  Pallas kernels  47 us (96%)
  local copies, waits for them, and re-layouts  1.62 us (3%)
    pallas_call x1, Pallas kernels, on_device(): pl.pallas_call(kernel, out_shape=jax.ShapeDtypeStruct(queries.shape, bf16...  47 us
    unnamed x1, local copies, waits for them, and re-layouts  1.62 us

profile of v4, /device:TPU:1, one launch (start us, length us, event | category | flops | bytes accessed | tf_op | source)
XLA Modules:
  0.0 48.6 jit_solution(13582899706165845135)
XLA Ops:
  0.0 47.0 %shard_map.64 = bf16[32,3072]{1,0:T(8,128)(2,1)} custom-call(bf16[32,3072]{1,0:T(8,128)(2,1)} %q_ref.1, bf16[32,3072]{1,0:T(8,128)(2,1)} %k_ref.1, bf16[32,3072]{1,0:T(8,128)(2,1)} %v_ref.1, s32[7]{0:T(128)} %offset_hbm.1, s32[7]{0:T(128)} %width_hbm.1, s32[7,8]{1,0:T(8,128)} %mask_hbm.1), custom_call_target="tpu_custom_call" | custom-call | tf_op jit(solution)/shard_map/pallas_call | solution.py:513
  47.0 1.6 %copy.8 = bf16[32,3072]{1,0:T(8,128)(2,1)} copy(bf16[32,3072]{1,0:T(8,128)(2,1)} %shard_map.64) | data formatting | bytes 393216

commit v5 on v4

--- a/solution.py
+++ b/solution.py
@@ -35,13 +35,13 @@
     def at(y_, z_, core_):
         return (y_ * 8 + z_) * 2 + core_
 
-    own_class = lax.rem(x + 8 - z, 4)
+    own_class = lax.rem(x + z, 4)
     frames = [16 * y + own_class + 4 * core + 8 * s for s in range(2)]
     home_class, _, home_core, home_slot = place(ctx)
     at_home = (home_class == own_class) & (home_core == core)
 
     def chip(class_, z_):
-        return lax.rem(class_ + z_, 4)
+        return lax.rem(class_ + 8 - z_, 4)
 
     mate_id = (at(y, z, 1 - core), x)
     up_id = (at(lax.rem(y + 1, 8), z, core), x)
@@ -427,8 +427,8 @@
     wait_mate(0)
     attend(near(0, 0), near(0, 1), near(1, 0, sets_mate))
     sends_2a(2, K)
+    sends_2a(2, V)
     sends_1b(2, K)
-    sends_2a(2, V)
     sends_1b(2, V)
     for h in (1, 2):
         send_y2(h, K, 1)

time: 48.8 us -> 48.7 us (level)
  Pallas kernels: 47 us -> 46.5 us
where the time goes in v5:
time: 48.7 us; the launch traced here: 48.2 us
  Pallas kernels  46.5 us (95%)
  local copies, waits for them, and re-layouts  1.62 us (3%)
    pallas_call x1, Pallas kernels, on_device(): pl.pallas_call(kernel, out_shape=jax.ShapeDtypeStruct(queries.shape, bf16...  46.5 us
    unnamed x1, local copies, waits for them, and re-layouts  1.62 us

profile of v5, /device:TPU:1, one launch (start us, length us, event | category | flops | bytes accessed | tf_op | source)
XLA Modules:
  0.0 48.2 jit_solution(1355867090891863973)
XLA Ops:
  0.0 46.5 %shard_map.64 = bf16[32,3072]{1,0:T(8,128)(2,1)} custom-call(bf16[32,3072]{1,0:T(8,128)(2,1)} %q_ref.1, bf16[32,3072]{1,0:T(8,128)(2,1)} %k_ref.1, bf16[32,3072]{1,0:T(8,128)(2,1)} %v_ref.1, s32[7]{0:T(128)} %offset_hbm.1, s32[7]{0:T(128)} %width_hbm.1, s32[7,8]{1,0:T(8,128)} %mask_hbm.1), custom_call_target="tpu_custom_call" | custom-call | tf_op jit(solution)/shard_map/pallas_call | solution.py:513
  46.5 1.6 %copy.8 = bf16[32,3072]{1,0:T(8,128)(2,1)} copy(bf16[32,3072]{1,0:T(8,128)(2,1)} %shard_map.64) | data formatting | bytes 393216
